TPU v7x, 32 devices: a whole 2x2x4 slice. The times are simulated.
32 devices in a mesh: gx: 4 (over y, core), gy: 4 (over z), gz: 2 (over x).
Axes of the slice: x: 2, y: 2, z: 4, core: 2. Of those that a mesh axis runs over, the one named last changes fastest.
Arguments:
- features: bfloat16 [32, 12, 32, 256], P(None, 'gx', 'gy', 'gz'), may hold values from -6 to 6
- edge_state: bfloat16 [3, 32, 12, 32, 256], P(None, None, 'gx', 'gy', 'gz'), may hold values from -6 to 6
- multiplicity: int32 [12, 32, 256], P('gx', 'gy', 'gz'), may hold values from 0 to 8
- edge_in: bfloat16 [3, 32, 96], replicated, may hold values from -0.625 to 0.625
- edge_out: bfloat16 [3, 32, 32], replicated, may hold values from -1 to 1
- edge_bias: float32 [3, 32], replicated, may hold values from -3 to 3
- node_in: bfloat16 [3, 32, 64], replicated, may hold values from -0.75 to 0.75
- node_out: bfloat16 [3, 32, 32], replicated, may hold values from -1 to 1
- node_bias: float32 [3, 32], replicated, may hold values from -3 to 3
Outputs:
- updated_features: bfloat16 [32, 12, 32, 256], P(None, 'gx', 'gy', 'gz')
All inputs are finite; a program needn't handle non-finite values.
Results may differ from a plain program's by a relative error of at most 0.009.
Values sent between devices are 32-bit elements; how exact they have to be, the bound alone decides.
A program may use at most 64 MiB of HBM per device.

v0:
```python
import jax
import jax.numpy as jnp
from jax import lax
from jax.sharding import PartitionSpec as P


def with_halo(block, sides, width):
    for axis, dim in sides:
        count = lax.axis_size(axis)
        forward = [(i, i + 1) for i in range(count - 1)]
        backward = [(target, source) for source, target in forward]
        low = lax.ppermute(
            lax.slice_in_dim(block, block.shape[dim] - width, None, axis=dim), axis, forward
        )
        high = lax.ppermute(lax.slice_in_dim(block, 0, width, axis=dim), axis, backward)
        block = jnp.concatenate([low, block, high], axis=dim)
    return block


def ahead(values, axis_pos):
    length = values.shape[axis_pos]
    remainder = lax.slice_in_dim(values, 1, length, axis=axis_pos)
    filler = jnp.zeros_like(lax.slice_in_dim(values, 0, 1, axis=axis_pos))
    return jnp.concatenate([remainder, filler], axis=axis_pos)


def behind(values, axis_pos):
    length = values.shape[axis_pos]
    remainder = lax.slice_in_dim(values, 0, length - 1, axis=axis_pos)
    filler = jnp.zeros_like(lax.slice_in_dim(values, 0, 1, axis=axis_pos))
    return jnp.concatenate([filler, remainder], axis=axis_pos)


def edge_layer(
    hidden_nodes, edges, counts, fluid, weight_in, weight_out, bias_in, spatial, count_dims
):
    channels = hidden_nodes.shape[0]
    shape = hidden_nodes.shape
    flat = hidden_nodes.reshape(channels, -1)
    stacked = jnp.concatenate(
        [weight_in[:, :channels], weight_in[:, channels : 2 * channels]], axis=0
    )
    projected = jnp.dot(stacked, flat, preferred_element_type=jnp.float32)
    own_part = projected[:channels].reshape(shape)
    other_part = projected[channels:].reshape(shape)
    bias = bias_in.reshape((channels,) + (1,) * (hidden_nodes.ndim - 1))
    incoming = jnp.zeros(shape, jnp.float32)
    updated = []
    for direction in range(3):
        edge_now = edges[direction]
        edge_term = jnp.dot(
            weight_in[:, 2 * channels :],
            edge_now.reshape(channels, -1),
            preferred_element_type=jnp.float32,
        ).reshape(shape)
        preact = own_part + ahead(other_part, spatial[direction]) + edge_term + bias
        edge_hidden = jax.nn.silu(preact).astype(jnp.bfloat16)
        message = jnp.dot(
            weight_out, edge_hidden.reshape(channels, -1), preferred_element_type=jnp.float32
        ).reshape(shape)
        updated.append((edge_now + message).astype(jnp.bfloat16))
        shared_count = jnp.minimum(counts, ahead(counts, count_dims[direction]))
        weight_edge = jnp.where(
            fluid & (shared_count > 0), 1.0 / jnp.maximum(shared_count, 1).astype(jnp.float32), 0.0
        )
        weighted = weight_edge[None] * message
        incoming = incoming + weighted + behind(weighted, spatial[direction])
    return (incoming, jnp.stack(updated))


def node_layer(hidden_nodes, incoming_rounded, weight_in, weight_out, bias_in):
    channels = hidden_nodes.shape[0]
    shape = hidden_nodes.shape
    node_pre = jnp.dot(
        weight_in[:, :channels],
        hidden_nodes.reshape(channels, -1),
        preferred_element_type=jnp.float32,
    )
    node_pre = node_pre + jnp.dot(
        weight_in[:, channels:],
        incoming_rounded.reshape(channels, -1),
        preferred_element_type=jnp.float32,
    )
    node_pre = node_pre + bias_in[:, None]
    node_hidden = jax.nn.silu(node_pre).astype(jnp.bfloat16)
    result = jnp.dot(weight_out, node_hidden, preferred_element_type=jnp.float32).reshape(shape)
    return (hidden_nodes + result).astype(jnp.bfloat16)


def fold_copies(padded, axis_pos):
    width = padded.shape[axis_pos] - 2
    inner = lax.slice_in_dim(padded, 1, width + 1, axis=axis_pos)
    lower = lax.index_in_dim(padded, 0, axis_pos, keepdims=False)
    upper = lax.index_in_dim(padded, width + 1, axis_pos, keepdims=False)
    front = (slice(None),) * axis_pos
    return inner.at[front + (0,)].add(lower).at[front + (width - 1,)].add(upper)


def sum_copies(incoming):
    padded = with_halo(incoming, (("gx", 1), ("gy", 2), ("gz", 3)), 1)
    return fold_copies(fold_copies(fold_copies(padded, 3), 2), 1)


def on_device(
    features, edge_state, multiplicity, edge_in, edge_out, edge_bias, node_in, node_out, node_bias
):
    fluid = multiplicity[1, 1, 1] > 0
    hidden_nodes = features
    edges = edge_state
    for layer_index in range(edge_in.shape[0]):
        incoming, edges = edge_layer(
            hidden_nodes,
            edges,
            multiplicity,
            fluid,
            edge_in[layer_index],
            edge_out[layer_index],
            edge_bias[layer_index],
            (1, 2, 3),
            (0, 1, 2),
        )
        incoming = sum_copies(incoming)
        hidden_nodes = node_layer(
            hidden_nodes,
            incoming.astype(jnp.bfloat16),
            node_in[layer_index],
            node_out[layer_index],
            node_bias[layer_index],
        )
    return hidden_nodes


def solution(mesh):
    placed = (
        P(None, "gx", "gy", "gz"),
        P(None, None, "gx", "gy", "gz"),
        P("gx", "gy", "gz"),
        P(),
        P(),
        P(),
        P(),
        P(),
        P(),
    )
    return jax.shard_map(
        on_device, mesh=mesh, in_specs=placed, out_specs=P(None, "gx", "gy", "gz"), check_vma=False
    )
```

profile of v0, /device:TPU:24, one launch (start us, length us, event | category | flops | bytes accessed | tf_op | source)
XLA Modules:
  0.0 135.7 jit_solution(7298060614104678964)
XLA Ops:
  0.8 1.2 fusion.67
  9.2 1.3 collective-permute-start.1
  10.5 3.0 %collective-permute-start = (f32[32,1,8,128]{3,2,1,0:T(8,128)S(1)}, f32[32,1,8,128]{3,2,1,0:T(8,128)S(1)}, u32[]{:S(2)}, u32[]{:S(2)}) collective-permute-start(f32[32,1,8,128]{3,2,1,0:T(8,128)S(1)} %get-tuple-element.252), channel_id=1, source_target_pairs={{0,8},{8,16},{16,24},{1,9},{9,17},{17,25},{2,10},{10,18},{18,26},{... | collective-permute-start | bytes 393224 | tf_op jit(solution)/shard_map/ppermute | solution.py:12
  15.4 0.9 pad_maximum_fusion.3
  16.3 2.2 %copy.163 = f32[32,5,8,128]{0,3,2,1:T(8,128)S(1)} copy(f32[32,5,8,128]{3,2,1,0:T(8,128)} %pad_maximum_fusion.3) | data formatting | bytes 1310720 | tf_op jit(solution)/shard_map/concatenate | solution.py:16
  18.5 2.4 %collective-permute-start.3 = (f32[32,5,1,128]{0,3,2,1:T(8,128)S(1)}, f32[32,5,1,128]{0,3,2,1:T(8,128)S(1)}, u32[]{:S(2)}, u32[]{:S(2)}) collective-permute-start(f32[32,5,1,128]{0,3,2,1:T(8,128)S(1)} %get-tuple-element.232), channel_id=1, source_target_pairs={{2,0},{4,2},{6,4},{3,1},{5,3},{7,5},{10,8},{12,10},{14,12},{11,9},... | collective-permute-start | bytes 245768 | tf_op jit(solution)/shard_map/ppermute | solution.py:15
  20.9 1.3 collective-permute-start.2
  22.5 6.3 %collective-permute-done.3 = f32[32,5,1,128]{0,3,2,1:T(8,128)S(1)} collective-permute-done((f32[32,5,1,128]{0,3,2,1:T(8,128)S(1)}, f32[32,5,1,128]{0,3,2,1:T(8,128)S(1)}, u32[]{:S(2)}, u32[]{:S(2)}) %collective-permute-start.3) | collective-permute-done | bytes 81952 | tf_op jit(solution)/shard_map/ppermute | solution.py:15
  28.8 4.5 %collective-permute-done.2 = f32[32,5,1,128]{0,3,2,1:T(8,128)S(1)} collective-permute-done((f32[32,5,1,128]{0,3,2,1:T(8,128)S(1)}, f32[32,5,1,128]{0,3,2,1:T(8,128)S(1)}, u32[]{:S(2)}, u32[]{:S(2)}) %collective-permute-start.2) | collective-permute-done | bytes 81952 | tf_op jit(solution)/shard_map/ppermute | solution.py:12
  33.3 2.0 %pad_maximum_fusion = f32[32,5,10,128]{0,3,2,1:T(8,128)S(1)} fusion(f32[32,5,1,128]{0,3,2,1:T(8,128)S(1)} %collective-permute-done.3, f32[32,5,8,128]{0,3,2,1:T(8,128)} %copy-done.1, f32[32,5,1,128]{0,3,2,1:T(8,128)S(1)} %collective-permute-done.2), kind=kLoop, calls=%fused_computation.9 | loop fusion | flops 409600 | bytes 1638400 | tf_op jit(solution)/shard_map/concatenate | solution.py:16
  35.3 3.4 %collective-permute-start.4 = (f32[32,5,10,1]{0,3,2,1:T(1,128)S(1)}, f32[32,5,10,1]{0,3,2,1:T(1,128)S(1)}, u32[]{:S(2)}, u32[]{:S(2)}) collective-permute-start(f32[32,5,10,1]{0,3,2,1:T(1,128)S(1)} %slice.930), channel_id=1, source_target_pairs={{0,1},{2,3},{4,5},{6,7},{8,9},{10,11},{12,13},{14,15},{16,17},{18,... | collective-permute-start | bytes 19208 | tf_op jit(solution)/shard_map/ppermute | solution.py:12
  39.0 1.2 collective-permute-done.4
  40.9 1.3 collective-permute-start.5
  43.3 0.8 copy.225
  44.9 0.8 scatter-add.60
  45.8 1.1 collective-permute-done.5
  55.1 1.3 collective-permute-start.7
  56.4 3.0 %collective-permute-start.6 = (f32[32,1,8,128]{3,2,1,0:T(8,128)S(1)}, f32[32,1,8,128]{3,2,1,0:T(8,128)S(1)}, u32[]{:S(2)}, u32[]{:S(2)}) collective-permute-start(f32[32,1,8,128]{3,2,1,0:T(8,128)S(1)} %get-tuple-element.250), channel_id=1, source_target_pairs={{0,8},{8,16},{16,24},{1,9},{9,17},{17,25},{2,10},{10,18},{18,26},{... | collective-permute-start | bytes 393224 | tf_op jit(solution)/shard_map/ppermute | solution.py:12
  59.4 1.0 collective-permute-done.6
  60.4 0.9 pad_maximum_fusion.4
  61.2 2.2 %copy.178 = f32[32,5,8,128]{0,3,2,1:T(8,128)S(1)} copy(f32[32,5,8,128]{3,2,1,0:T(8,128)} %pad_maximum_fusion.4) | data formatting | bytes 1310720 | tf_op jit(solution)/shard_map/concatenate | solution.py:16
  63.5 2.4 %collective-permute-start.9 = (f32[32,5,1,128]{0,3,2,1:T(8,128)S(1)}, f32[32,5,1,128]{0,3,2,1:T(8,128)S(1)}, u32[]{:S(2)}, u32[]{:S(2)}) collective-permute-start(f32[32,5,1,128]{0,3,2,1:T(8,128)S(1)} %get-tuple-element.230), channel_id=1, source_target_pairs={{2,0},{4,2},{6,4},{3,1},{5,3},{7,5},{10,8},{12,10},{14,12},{11,9},... | collective-permute-start | bytes 245768 | tf_op jit(solution)/shard_map/ppermute | solution.py:15
  65.9 1.3 collective-permute-start.8
  67.2 1.2 convolution_bitcast_fusion.7
  68.5 5.5 %collective-permute-done.9 = f32[32,5,1,128]{0,3,2,1:T(8,128)S(1)} collective-permute-done((f32[32,5,1,128]{0,3,2,1:T(8,128)S(1)}, f32[32,5,1,128]{0,3,2,1:T(8,128)S(1)}, u32[]{:S(2)}, u32[]{:S(2)}) %collective-permute-start.9) | collective-permute-done | bytes 81952 | tf_op jit(solution)/shard_map/ppermute | solution.py:15
  74.0 4.1 %collective-permute-done.8 = f32[32,5,1,128]{0,3,2,1:T(8,128)S(1)} collective-permute-done((f32[32,5,1,128]{0,3,2,1:T(8,128)S(1)}, f32[32,5,1,128]{0,3,2,1:T(8,128)S(1)}, u32[]{:S(2)}, u32[]{:S(2)}) %collective-permute-start.8) | collective-permute-done | bytes 81952 | tf_op jit(solution)/shard_map/ppermute | solution.py:12
  78.1 2.0 %pad_maximum_fusion.1 = f32[32,5,10,128]{0,3,2,1:T(8,128)S(1)} fusion(f32[32,5,1,128]{0,3,2,1:T(8,128)S(1)} %collective-permute-done.9, f32[32,5,8,128]{0,3,2,1:T(8,128)} %copy-done, f32[32,5,1,128]{0,3,2,1:T(8,128)S(1)} %collective-permute-done.8), kind=kLoop, calls=%fused_computation.10 | loop fusion | flops 409600 | bytes 1638400 | tf_op jit(solution)/shard_map/concatenate | solution.py:16
  80.1 4.1 %collective-permute-start.10 = (f32[32,5,10,1]{0,3,2,1:T(1,128)S(1)}, f32[32,5,10,1]{0,3,2,1:T(1,128)S(1)}, u32[]{:S(2)}, u32[]{:S(2)}) collective-permute-start(f32[32,5,10,1]{0,3,2,1:T(1,128)S(1)} %slice.960), channel_id=1, source_target_pairs={{0,1},{2,3},{4,5},{6,7},{8,9},{10,11},{12,13},{14,15},{16,17},{18,... | collective-permute-start | bytes 19208 | tf_op jit(solution)/shard_map/ppermute | solution.py:12
  84.5 1.2 collective-permute-done.10
  85.8 1.3 collective-permute-start.11
  87.4 0.8 copy.235
  88.2 0.8 copy.238
  89.0 0.8 copy.241
  90.0 1.5 %collective-permute-done.11 = f32[32,5,10,1]{0,3,2,1:T(1,128)S(1)} collective-permute-done((f32[32,5,10,1]{0,3,2,1:T(1,128)S(1)}, f32[32,5,10,1]{0,3,2,1:T(1,128)S(1)}, u32[]{:S(2)}, u32[]{:S(2)}) %collective-permute-start.11) | collective-permute-done | bytes 6432 | tf_op jit(solution)/shard_map/ppermute | solution.py:15
  97.6 1.3 collective-permute-start.13
  98.9 3.0 %collective-permute-start.12 = (f32[32,1,8,128]{3,2,1,0:T(8,128)S(1)}, f32[32,1,8,128]{3,2,1,0:T(8,128)S(1)}, u32[]{:S(2)}, u32[]{:S(2)}) collective-permute-start(f32[32,1,8,128]{3,2,1,0:T(8,128)S(1)} %get-tuple-element.248), channel_id=1, source_target_pairs={{0,8},{8,16},{16,24},{1,9},{9,17},{17,25},{2,10},{10,18},{18,26},{... | collective-permute-start | bytes 393224 | tf_op jit(solution)/shard_map/ppermute | solution.py:12
  101.9 1.0 collective-permute-done.12
  102.9 1.3 copy.193
  104.2 2.4 %collective-permute-start.15 = (f32[32,5,1,128]{0,3,2,1:T(8,128)S(1)}, f32[32,5,1,128]{0,3,2,1:T(8,128)S(1)}, u32[]{:S(2)}, u32[]{:S(2)}) collective-permute-start(f32[32,5,1,128]{0,3,2,1:T(8,128)S(1)} %get-tuple-element.228), channel_id=1, source_target_pairs={{2,0},{4,2},{6,4},{3,1},{5,3},{7,5},{10,8},{12,10},{14,12},{11,9},... | collective-permute-start | bytes 245768 | tf_op jit(solution)/shard_map/ppermute | solution.py:15
  106.6 1.3 collective-permute-start.14
  107.9 6.8 %collective-permute-done.15 = f32[32,5,1,128]{0,3,2,1:T(8,128)S(1)} collective-permute-done((f32[32,5,1,128]{0,3,2,1:T(8,128)S(1)}, f32[32,5,1,128]{0,3,2,1:T(8,128)S(1)}, u32[]{:S(2)}, u32[]{:S(2)}) %collective-permute-start.15) | collective-permute-done | bytes 81952 | tf_op jit(solution)/shard_map/ppermute | solution.py:15
  114.7 4.1 %collective-permute-done.14 = f32[32,5,1,128]{0,3,2,1:T(8,128)S(1)} collective-permute-done((f32[32,5,1,128]{0,3,2,1:T(8,128)S(1)}, f32[32,5,1,128]{0,3,2,1:T(8,128)S(1)}, u32[]{:S(2)}, u32[]{:S(2)}) %collective-permute-start.14) | collective-permute-done | bytes 81952 | tf_op jit(solution)/shard_map/ppermute | solution.py:12
  118.8 2.0 %pad_maximum_fusion.2 = f32[32,5,10,128]{0,3,2,1:T(8,128)S(1)} fusion(f32[32,5,1,128]{0,3,2,1:T(8,128)S(1)} %collective-permute-done.15, f32[32,5,8,128]{0,3,2,1:T(8,128)} %copy-done.2, f32[32,5,1,128]{0,3,2,1:T(8,128)S(1)} %collective-permute-done.14), kind=kLoop, calls=%fused_computation.11 | loop fusion | flops 409600 | bytes 1638400 | tf_op jit(solution)/shard_map/concatenate | solution.py:16
  120.8 3.0 %collective-permute-start.16 = (f32[32,5,10,1]{0,3,2,1:T(1,128)S(1)}, f32[32,5,10,1]{0,3,2,1:T(1,128)S(1)}, u32[]{:S(2)}, u32[]{:S(2)}) collective-permute-start(f32[32,5,10,1]{0,3,2,1:T(1,128)S(1)} %slice.990), channel_id=1, source_target_pairs={{0,1},{2,3},{4,5},{6,7},{8,9},{10,11},{12,13},{14,15},{16,17},{18,... | collective-permute-start | bytes 19208 | tf_op jit(solution)/shard_map/ppermute | solution.py:12
  123.9 1.5 %collective-permute-done.16 = f32[32,5,10,1]{0,3,2,1:T(1,128)S(1)} collective-permute-done((f32[32,5,10,1]{0,3,2,1:T(1,128)S(1)}, f32[32,5,10,1]{0,3,2,1:T(1,128)S(1)}, u32[]{:S(2)}, u32[]{:S(2)}) %collective-permute-start.16) | collective-permute-done | bytes 6432 | tf_op jit(solution)/shard_map/ppermute | solution.py:12
  125.5 1.3 collective-permute-start.17
  126.9 4.4 %collective-permute-done.17 = f32[32,5,10,1]{0,3,2,1:T(1,128)} collective-permute-done((f32[32,5,10,1]{0,3,2,1:T(1,128)S(1)}, f32[32,5,10,1]{0,3,2,1:T(1,128)}, u32[]{:S(2)}, u32[]{:S(2)}) %collective-permute-start.17) | collective-permute-done | bytes 6432 | tf_op jit(solution)/shard_map/ppermute | solution.py:15
  133.7 1.1 convolution_bitcast_fusion.1
  (256 shorter events, 29.7 us)
Async XLA Ops:
  0.0 2.4 %copy-start.32 = (s32[3,8,128]{2,1,0:T(8,128)S(1)}, s32[3,8,128]{2,1,0:T(8,128)}, u32[]{:S(2)}) copy-start(s32[3,8,128]{2,1,0:T(8,128)} %param.47) | copy-start | bytes 36868
  2.0 1.3 copy-start.30
  2.1 1.3 copy-start.43
  3.4 18.8 %copy-start.17 = (bf16[32,3072]{1,0:T(8,128)(2,1)}, bf16[32,3072]{1,0:T(8,128)(2,1)S(1)}, u32[]{:S(2)}) copy-start(bf16[32,3072]{1,0:T(8,128)(2,1)S(1)} %reshape_squeeze.12) | copy-start | bytes 589828
  4.7 37.5 %copy-start.15 = (bf16[32,3072]{1,0:T(8,128)(2,1)}, bf16[32,3072]{1,0:T(8,128)(2,1)S(1)}, u32[]{:S(2)}) copy-start(bf16[32,3072]{1,0:T(8,128)(2,1)S(1)} %reshape_squeeze.14) | copy-start | bytes 589828
  5.4 16.8 %copy-start.9 = (f32[3072,32]{0,1:T(8,128)}, f32[3072,32]{0,1:T(8,128)S(1)}, u32[]{:S(2)}) copy-start(f32[3072,32]{0,1:T(8,128)S(1)} %fusion.64) | copy-start | bytes 1179652
  6.5 1.6 %copy-start.18 = (bf16[32,3072]{1,0:T(8,128)(2,1)}, bf16[32,3072]{1,0:T(8,128)(2,1)S(1)}, u32[]{:S(2)}) copy-start(bf16[32,3072]{1,0:T(8,128)(2,1)S(1)} %reshape_squeeze.13) | copy-start | bytes 589828
  6.5 2.2 %copy-start.33 = (s32[3,8,128]{2,1,0:T(8,128)S(1)}, s32[3,8,128]{2,1,0:T(8,128)}, u32[]{:S(2)}) copy-start(s32[3,8,128]{2,1,0:T(8,128)} %param.47) | copy-start | bytes 36868
  6.6 2.2 %slice-start = ((s32[3,8,128]{2,1,0:T(8,128)}), s32[2,8,128]{2,1,0:T(8,128)S(1)}, s32[]{:S(2)}) async-start(s32[3,8,128]{2,1,0:T(8,128)} %param.47), calls=%async_computation | async-start | bytes 16384 | tf_op jit(solution)/shard_map/slice | solution.py:22
  8.8 4.7 %copy-start.41 = (bf16[3,32,64]{2,1,0:T(8,128)(2,1)S(1)}, bf16[3,32,64]{2,1,0:T(8,128)(2,1)}, u32[]{:S(2)}) copy-start(bf16[3,32,64]{2,1,0:T(8,128)(2,1)} %param.51) | copy-start | bytes 36868
  8.8 6.0 %copy-start.44 = (f32[3,32]{1,0:T(4,128)S(1)}, f32[3,32]{1,0:T(4,128)}, u32[]{:S(2)}) copy-start(f32[3,32]{1,0:T(4,128)} %param.53) | copy-start | bytes 1156
  9.2 6.2 %collective-permute-start.1 = (f32[32,1,8,128]{3,2,1,0:T(8,128)S(1)}, f32[32,1,8,128]{3,2,1,0:T(8,128)S(1)}, u32[]{:S(2)}, u32[]{:S(2)}) collective-permute-start(f32[32,1,8,128]{3,2,1,0:T(8,128)S(1)} %get-tuple-element.253), channel_id=1, source_target_pairs={{8,0},{16,8},{24,16},{9,1},{17,9},{25,17},{10,2},{18,10},{26,18},{... | collective-permute-start | bytes 393224 | tf_op jit(solution)/shard_map/ppermute | solution.py:15
  10.5 4.9 %collective-permute-start = (f32[32,1,8,128]{3,2,1,0:T(8,128)S(1)}, f32[32,1,8,128]{3,2,1,0:T(8,128)S(1)}, u32[]{:S(2)}, u32[]{:S(2)}) collective-permute-start(f32[32,1,8,128]{3,2,1,0:T(8,128)S(1)} %get-tuple-element.252), channel_id=1, source_target_pairs={{0,8},{8,16},{16,24},{1,9},{9,17},{17,25},{2,10},{10,18},{18,26},{... | collective-permute-start | bytes 393224 | tf_op jit(solution)/shard_map/ppermute | solution.py:12
  18.5 10.3 %copy-start.1 = (f32[32,5,8,128]{0,3,2,1:T(8,128)}, f32[32,5,8,128]{0,3,2,1:T(8,128)S(1)}, u32[]{:S(2)}) copy-start(f32[32,5,8,128]{0,3,2,1:T(8,128)S(1)} %copy.163) | copy-start | bytes 1966084
  18.5 10.2 %collective-permute-start.3 = (f32[32,5,1,128]{0,3,2,1:T(8,128)S(1)}, f32[32,5,1,128]{0,3,2,1:T(8,128)S(1)}, u32[]{:S(2)}, u32[]{:S(2)}) collective-permute-start(f32[32,5,1,128]{0,3,2,1:T(8,128)S(1)} %get-tuple-element.232), channel_id=1, source_target_pairs={{2,0},{4,2},{6,4},{3,1},{5,3},{7,5},{10,8},{12,10},{14,12},{11,9},... | collective-permute-start | bytes 245768 | tf_op jit(solution)/shard_map/ppermute | solution.py:15
  20.9 12.4 %collective-permute-start.2 = (f32[32,5,1,128]{0,3,2,1:T(8,128)S(1)}, f32[32,5,1,128]{0,3,2,1:T(8,128)S(1)}, u32[]{:S(2)}, u32[]{:S(2)}) collective-permute-start(f32[32,5,1,128]{0,3,2,1:T(8,128)S(1)} %get-tuple-element.231), channel_id=1, source_target_pairs={{0,2},{2,4},{4,6},{1,3},{3,5},{5,7},{8,10},{10,12},{12,14},{9,11},... | collective-permute-start | bytes 245768 | tf_op jit(solution)/shard_map/ppermute | solution.py:12
  22.5 16.3 %copy-start.7 = (f32[3072,32]{0,1:T(8,128)S(1)}, f32[3072,32]{0,1:T(8,128)}, u32[]{:S(2)}) copy-start(f32[3072,32]{0,1:T(8,128)} %copy-done.6) | copy-start | bytes 1179652
  22.5 16.3 %copy-start.19 = (bf16[32,3072]{1,0:T(8,128)(2,1)S(1)}, bf16[32,3072]{1,0:T(8,128)(2,1)}, u32[]{:S(2)}) copy-start(bf16[32,3072]{1,0:T(8,128)(2,1)} %copy-done.18) | copy-start | bytes 589828
  22.5 19.7 %copy-start.4 = (f32[3072,32]{0,1:T(8,128)S(1)}, f32[3072,32]{0,1:T(8,128)}, u32[]{:S(2)}) copy-start(f32[3072,32]{0,1:T(8,128)} %copy-done.3) | copy-start | bytes 1179652
  35.3 4.9 %collective-permute-start.4 = (f32[32,5,10,1]{0,3,2,1:T(1,128)S(1)}, f32[32,5,10,1]{0,3,2,1:T(1,128)S(1)}, u32[]{:S(2)}, u32[]{:S(2)}) collective-permute-start(f32[32,5,10,1]{0,3,2,1:T(1,128)S(1)} %slice.930), channel_id=1, source_target_pairs={{0,1},{2,3},{4,5},{6,7},{8,9},{10,11},{12,13},{14,15},{16,17},{18,... | collective-permute-start | bytes 19208 | tf_op jit(solution)/shard_map/ppermute | solution.py:12
  40.9 6.0 %collective-permute-start.5 = (f32[32,5,10,1]{0,3,2,1:T(1,128)}, f32[32,5,10,1]{0,3,2,1:T(1,128)}, u32[]{:S(2)}, u32[]{:S(2)}) collective-permute-start(f32[32,5,10,1]{0,3,2,1:T(1,128)} %get-tuple-element.225), channel_id=1, source_target_pairs={{1,0},{3,2},{5,4},{7,6},{9,8},{11,10},{13,12},{15,14},{17,16},{19,... | collective-permute-start | bytes 19208 | tf_op jit(solution)/shard_map/ppermute | solution.py:15
  48.7 1.3 copy-start.39
  48.7 1.3 copy-start.40
  50.4 1.2 copy-start.28
  55.1 4.3 %collective-permute-start.7 = (f32[32,1,8,128]{3,2,1,0:T(8,128)S(1)}, f32[32,1,8,128]{3,2,1,0:T(8,128)S(1)}, u32[]{:S(2)}, u32[]{:S(2)}) collective-permute-start(f32[32,1,8,128]{3,2,1,0:T(8,128)S(1)} %get-tuple-element.251), channel_id=1, source_target_pairs={{8,0},{16,8},{24,16},{9,1},{17,9},{25,17},{10,2},{18,10},{26,18},{... | collective-permute-start | bytes 393224 | tf_op jit(solution)/shard_map/ppermute | solution.py:15
  56.4 4.0 %collective-permute-start.6 = (f32[32,1,8,128]{3,2,1,0:T(8,128)S(1)}, f32[32,1,8,128]{3,2,1,0:T(8,128)S(1)}, u32[]{:S(2)}, u32[]{:S(2)}) collective-permute-start(f32[32,1,8,128]{3,2,1,0:T(8,128)S(1)} %get-tuple-element.250), channel_id=1, source_target_pairs={{0,8},{8,16},{16,24},{1,9},{9,17},{17,25},{2,10},{10,18},{18,26},{... | collective-permute-start | bytes 393224 | tf_op jit(solution)/shard_map/ppermute | solution.py:12
  61.2 6.0 %copy-start.10 = (f32[3072,32]{0,1:T(8,128)S(1)}, f32[3072,32]{0,1:T(8,128)}, u32[]{:S(2)}) copy-start(f32[3072,32]{0,1:T(8,128)} %copy-done.9) | copy-start | bytes 1179652
  63.5 10.5 %copy-start = (f32[32,5,8,128]{0,3,2,1:T(8,128)}, f32[32,5,8,128]{0,3,2,1:T(8,128)S(1)}, u32[]{:S(2)}) copy-start(f32[32,5,8,128]{0,3,2,1:T(8,128)S(1)} %copy.178) | copy-start | bytes 1966084
  63.5 10.4 %collective-permute-start.9 = (f32[32,5,1,128]{0,3,2,1:T(8,128)S(1)}, f32[32,5,1,128]{0,3,2,1:T(8,128)S(1)}, u32[]{:S(2)}, u32[]{:S(2)}) collective-permute-start(f32[32,5,1,128]{0,3,2,1:T(8,128)S(1)} %get-tuple-element.230), channel_id=1, source_target_pairs={{2,0},{4,2},{6,4},{3,1},{5,3},{7,5},{10,8},{12,10},{14,12},{11,9},... | collective-permute-start | bytes 245768 | tf_op jit(solution)/shard_map/ppermute | solution.py:15
  65.9 12.2 %collective-permute-start.8 = (f32[32,5,1,128]{0,3,2,1:T(8,128)S(1)}, f32[32,5,1,128]{0,3,2,1:T(8,128)S(1)}, u32[]{:S(2)}, u32[]{:S(2)}) collective-permute-start(f32[32,5,1,128]{0,3,2,1:T(8,128)S(1)} %get-tuple-element.229), channel_id=1, source_target_pairs={{0,2},{2,4},{4,6},{1,3},{3,5},{5,7},{8,10},{10,12},{12,14},{9,11},... | collective-permute-start | bytes 245768 | tf_op jit(solution)/shard_map/ppermute | solution.py:12
  68.4 15.9 %copy-start.8 = (f32[3072,32]{0,1:T(8,128)S(1)}, f32[3072,32]{0,1:T(8,128)}, u32[]{:S(2)}) copy-start(f32[3072,32]{0,1:T(8,128)} %copy-done.6) | copy-start | bytes 1179652
  68.4 15.9 %copy-start.14 = (f32[3072,32]{0,1:T(8,128)S(1)}, f32[3072,32]{0,1:T(8,128)}, u32[]{:S(2)}) copy-start(f32[3072,32]{0,1:T(8,128)} %copy-done.13) | copy-start | bytes 1179652
  68.4 15.9 %copy-start.20 = (bf16[32,3072]{1,0:T(8,128)(2,1)S(1)}, bf16[32,3072]{1,0:T(8,128)(2,1)}, u32[]{:S(2)}) copy-start(bf16[32,3072]{1,0:T(8,128)(2,1)} %copy-done.18) | copy-start | bytes 589828
  68.4 18.7 %copy-start.5 = (f32[3072,32]{0,1:T(8,128)S(1)}, f32[3072,32]{0,1:T(8,128)}, u32[]{:S(2)}) copy-start(f32[3072,32]{0,1:T(8,128)} %copy-done.3) | copy-start | bytes 1179652
  68.4 18.7 %copy-start.12 = (f32[3072,32]{0,1:T(8,128)S(1)}, f32[3072,32]{0,1:T(8,128)}, u32[]{:S(2)}) copy-start(f32[3072,32]{0,1:T(8,128)} %copy-done.11) | copy-start | bytes 1179652
  68.4 18.7 %copy-start.16 = (bf16[32,3072]{1,0:T(8,128)(2,1)S(1)}, bf16[32,3072]{1,0:T(8,128)(2,1)}, u32[]{:S(2)}) copy-start(bf16[32,3072]{1,0:T(8,128)(2,1)} %copy-done.15) | copy-start | bytes 589828
  80.1 5.6 %collective-permute-start.10 = (f32[32,5,10,1]{0,3,2,1:T(1,128)S(1)}, f32[32,5,10,1]{0,3,2,1:T(1,128)S(1)}, u32[]{:S(2)}, u32[]{:S(2)}) collective-permute-start(f32[32,5,10,1]{0,3,2,1:T(1,128)S(1)} %slice.960), channel_id=1, source_target_pairs={{0,1},{2,3},{4,5},{6,7},{8,9},{10,11},{12,13},{14,15},{16,17},{18,... | collective-permute-start | bytes 19208 | tf_op jit(solution)/shard_map/ppermute | solution.py:12
  85.8 5.7 %collective-permute-start.11 = (f32[32,5,10,1]{0,3,2,1:T(1,128)S(1)}, f32[32,5,10,1]{0,3,2,1:T(1,128)S(1)}, u32[]{:S(2)}, u32[]{:S(2)}) collective-permute-start(f32[32,5,10,1]{0,3,2,1:T(1,128)S(1)} %get-tuple-element.223), channel_id=1, source_target_pairs={{1,0},{3,2},{5,4},{7,6},{9,8},{11,10},{13,12},{15,14},{17,16},{19,... | collective-permute-start | bytes 19208 | tf_op jit(solution)/shard_map/ppermute | solution.py:15
  92.7 1.3 copy-start.37
  92.7 1.3 copy-start.38
  94.4 1.2 copy-start.25
  97.6 4.3 %collective-permute-start.13 = (f32[32,1,8,128]{3,2,1,0:T(8,128)S(1)}, f32[32,1,8,128]{3,2,1,0:T(8,128)S(1)}, u32[]{:S(2)}, u32[]{:S(2)}) collective-permute-start(f32[32,1,8,128]{3,2,1,0:T(8,128)S(1)} %get-tuple-element.249), channel_id=1, source_target_pairs={{8,0},{16,8},{24,16},{9,1},{17,9},{25,17},{10,2},{18,10},{26,18},{... | collective-permute-start | bytes 393224 | tf_op jit(solution)/shard_map/ppermute | solution.py:15
  98.9 4.0 %collective-permute-start.12 = (f32[32,1,8,128]{3,2,1,0:T(8,128)S(1)}, f32[32,1,8,128]{3,2,1,0:T(8,128)S(1)}, u32[]{:S(2)}, u32[]{:S(2)}) collective-permute-start(f32[32,1,8,128]{3,2,1,0:T(8,128)S(1)} %get-tuple-element.248), channel_id=1, source_target_pairs={{0,8},{8,16},{16,24},{1,9},{9,17},{17,25},{2,10},{10,18},{18,26},{... | collective-permute-start | bytes 393224 | tf_op jit(solution)/shard_map/ppermute | solution.py:12
  104.2 10.5 %copy-start.2 = (f32[32,5,8,128]{0,3,2,1:T(8,128)}, f32[32,5,8,128]{0,3,2,1:T(8,128)S(1)}, u32[]{:S(2)}) copy-start(f32[32,5,8,128]{0,3,2,1:T(8,128)S(1)} %copy.193) | copy-start | bytes 1966084
  104.2 10.4 %collective-permute-start.15 = (f32[32,5,1,128]{0,3,2,1:T(8,128)S(1)}, f32[32,5,1,128]{0,3,2,1:T(8,128)S(1)}, u32[]{:S(2)}, u32[]{:S(2)}) collective-permute-start(f32[32,5,1,128]{0,3,2,1:T(8,128)S(1)} %get-tuple-element.228), channel_id=1, source_target_pairs={{2,0},{4,2},{6,4},{3,1},{5,3},{7,5},{10,8},{12,10},{14,12},{11,9},... | collective-permute-start | bytes 245768 | tf_op jit(solution)/shard_map/ppermute | solution.py:15
  106.6 12.2 %collective-permute-start.14 = (f32[32,5,1,128]{0,3,2,1:T(8,128)S(1)}, f32[32,5,1,128]{0,3,2,1:T(8,128)S(1)}, u32[]{:S(2)}, u32[]{:S(2)}) collective-permute-start(f32[32,5,1,128]{0,3,2,1:T(8,128)S(1)} %get-tuple-element.227), channel_id=1, source_target_pairs={{0,2},{2,4},{4,6},{1,3},{3,5},{5,7},{8,10},{10,12},{12,14},{9,11},... | collective-permute-start | bytes 245768 | tf_op jit(solution)/shard_map/ppermute | solution.py:12
  120.8 4.6 %collective-permute-start.16 = (f32[32,5,10,1]{0,3,2,1:T(1,128)S(1)}, f32[32,5,10,1]{0,3,2,1:T(1,128)S(1)}, u32[]{:S(2)}, u32[]{:S(2)}) collective-permute-start(f32[32,5,10,1]{0,3,2,1:T(1,128)S(1)} %slice.990), channel_id=1, source_target_pairs={{0,1},{2,3},{4,5},{6,7},{8,9},{10,11},{12,13},{14,15},{16,17},{18,... | collective-permute-start | bytes 19208 | tf_op jit(solution)/shard_map/ppermute | solution.py:12
  125.5 5.8 %collective-permute-start.17 = (f32[32,5,10,1]{0,3,2,1:T(1,128)S(1)}, f32[32,5,10,1]{0,3,2,1:T(1,128)}, u32[]{:S(2)}, u32[]{:S(2)}) collective-permute-start(f32[32,5,10,1]{0,3,2,1:T(1,128)S(1)} %get-tuple-element.221), channel_id=1, source_target_pairs={{1,0},{3,2},{5,4},{7,6},{9,8},{11,10},{13,12},{15,14},{17,16},{19,... | collective-permute-start | bytes 19208 | tf_op jit(solution)/shard_map/ppermute | solution.py:15
  (20 other events, 18.1 us)
where the time goes:
time: 137 us; the launch traced here: 136 us
  waiting for transfers between devices  44.3 us (32%)
  starting transfers between devices  38.4 us (28%)
  local copies, waits for them, and re-layouts  26.8 us (20%)
  other arithmetic  14.1 us (10%)
  matrix products  9.69 us (7%)
  between operations  2.35 us (2%)
    ppermute x9, waiting for transfers between devices, with_halo(): lax.ppermute(lax.slice_in_dim(block, 0, width, axis=dim), axis, backward)  25.6 us
    ppermute x9, starting transfers between devices, with_halo(): lax.ppermute(lax.slice_in_dim(block, block.shape[dim] - width, None, axis...  23.5 us
    ppermute x9, waiting for transfers between devices, with_halo(): lax.ppermute(lax.slice_in_dim(block, block.shape[dim] - width, None, axis...  18.7 us
    ppermute x9, starting transfers between devices, with_halo(): lax.ppermute(lax.slice_in_dim(block, 0, width, axis=dim), axis, backward)  14.8 us
    unnamed x137, local copies, waits for them, and re-layouts  12.6 us
    concatenate x6, other arithmetic, with_halo(): block = jnp.concatenate([low, block, high], axis=dim)  7.77 us
    concatenate x3, local copies, waits for them, and re-layouts, with_halo(): block = jnp.concatenate([low, block, high], axis=dim)  5.65 us
    dot_general x9, matrix products, edge_layer(): jnp.dot(weight_in[:, 2 * channels:], edge_now.reshape(channels, -1), pref...  3.4 us
  transfers between devices with their start and end apart: 18, of which 14 were waited for; matrix products, arithmetic and copies ran while one was open for 8% of the time, Pallas kernels for 0%

commit v1 on v0

v1 whole, which is shorter than its diff:
```python
import functools
import itertools

import jax
import jax.numpy as jnp
from jax import lax
from jax.experimental import pallas as pl
from jax.experimental.pallas import tpu as pltpu
from jax.sharding import PartitionSpec as P

MESH = pl.DeviceIdType.MESH
AXES = ("gx", "gy", "gz")
F32, BF16 = jnp.float32, jnp.bfloat16
WAYS = [way for way in itertools.product((-1, 0, 1), repeat=3) if any(way)]


def iota(shape, dim):
    return lax.broadcasted_iota(jnp.int32, shape, dim)


def dot(a, b):
    return jnp.dot(a, b, preferred_element_type=F32)


def silu_of_half(half):
    return half + half * jnp.tanh(half)


def split(values):
    high = values.astype(BF16)
    return high, (values - high.astype(F32)).astype(BF16)


def kernel(
    sizes,
    layers,
    feat_ref, edge_ref, mult_ref, win_ref, wout_ref, bin_ref, nin_ref, nout_ref, bnode_ref,
    out_ref,
    h_s, hz_s, e_s, w_s, p_s, inc_s, mat_e, mat_o, mat_n, mat_no, bias_e, bias_n,
    ysend, zsend, xrx, yrx, xyrx, zrx, send_sem, recv_sem,
):
    chans, cx, cy, cz = feat_ref.shape
    rows = chans * cy
    halves = rows // 128
    last = cx - 1
    slots = p_s.shape[0]
    zrows = zsend.shape[2]
    place = [lax.axis_index(axis) for axis in AXES]

    def exists(way):
        there = None
        for pos, step, size in zip(place, way, sizes):
            if step == 0:
                continue
            here = pos > 0 if step < 0 else pos < size - 1
            there = here if there is None else there & here
        return there

    def device(way):
        return {axis: pos + step for axis, pos, step in zip(AXES, place, way)}

    def back(way):
        return tuple(-step for step in way)

    ways = [way for way in WAYS if all(step == 0 or size > 1 for step, size in zip(way, sizes))]

    xrx[...] = jnp.zeros_like(xrx)
    yrx[...] = jnp.zeros_like(yrx)
    xyrx[...] = jnp.zeros_like(xyrx)
    zrx[...] = jnp.zeros_like(zrx)

    barrier = pltpu.get_barrier_semaphore()
    for way in ways:
        @pl.when(exists(way))
        def _():
            pl.semaphore_signal(barrier, inc=1, device_id=device(way), device_id_type=MESH)

    spread = (iota((rows, chans), 0) // cy == iota((rows, chans), 1)).astype(F32).astype(BF16)
    row_y, col_y = iota((rows, rows), 0) % cy, iota((rows, rows), 1) % cy
    same_y, next_y = row_y == col_y, row_y + 1 == col_y

    def widen(tall, part):
        width = tall.shape[1]
        pick = iota((width, rows), 0) == part * chans + iota((width, rows), 1) // cy
        return dot(tall, pick.astype(F32).astype(BF16))

    def build(layer):
        tall = dot(spread, win_ref[layer]).astype(BF16)
        own, other, edge = (0.5 * widen(tall, part) for part in range(3))
        own = jnp.where(same_y, own, 0.0)
        mat_e[layer, :, 0:rows] = own.astype(BF16)
        mat_e[layer, :, rows : 2 * rows] = jnp.where(same_y, other, 0.0).astype(BF16)
        mat_e[layer, :, 2 * rows : 3 * rows] = jnp.where(same_y, edge, 0.0).astype(BF16)
        mat_e[layer, :, 3 * rows :] = jnp.where(next_y, other, own).astype(BF16)
        tall = dot(spread, wout_ref[layer]).astype(BF16)
        mat_o[layer] = jnp.where(same_y, widen(tall, 0), 0.0).astype(BF16)
        tall = dot(spread, nin_ref[layer]).astype(BF16)
        for part in range(2):
            mat_n[layer, :, part * rows : (part + 1) * rows] = jnp.where(
                same_y, 0.5 * widen(tall, part), 0.0
            ).astype(BF16)
        tall = dot(spread, nout_ref[layer]).astype(BF16)
        mat_no[layer] = jnp.where(same_y, widen(tall, 0), 0.0).astype(BF16)
        mine = iota((rows, chans), 0) // cy == iota((rows, chans), 1)
        for source, target in ((bin_ref, bias_e), (bnode_ref, bias_n)):
            column = jnp.sum(
                jnp.where(mine, source[pl.ds(layer, 1), :], 0.0), axis=1, keepdims=True
            )
            target[layer] = jnp.broadcast_to(0.5 * column, (rows, cz))

    def build_step(layer, carry):
        build(layer)
        return carry

    lax.fori_loop(0, layers, build_step, 0)

    fluid = mult_ref[1, 1:2, 1:2] > 0
    zeros = jnp.zeros((cy, cz), jnp.int32)
    for x in range(cx):
        count = mult_ref[x]
        ahead = (
            mult_ref[x + 1] if x < last else zeros,
            jnp.where(iota((cy, cz), 0) < cy - 1, pltpu.roll(count, cy - 1, 0), 0),
            jnp.where(iota((cy, cz), 1) < cz - 1, pltpu.roll(count, cz - 1, 1), 0),
        )
        for d in range(3):
            shared = jnp.minimum(count, ahead[d])
            w_s[d, x] = jnp.where(
                fluid & (shared > 0), 1.0 / jnp.maximum(shared, 1).astype(F32), 0.0
            )

    before_end = iota((rows, cz), 1) < cz - 1

    def keep_nodes(x, values):
        h_s[x] = values.astype(BF16)
        hz_s[x] = jnp.where(before_end, pltpu.roll(values, cz - 1, 1), 0.0).astype(BF16)

    for x in range(cx):
        keep_nodes(x, feat_ref[:, x].astype(F32).reshape(rows, cz))
        for d in range(3):
            e_s[d, x] = edge_ref[d, :, x].astype(F32).reshape(rows, cz).astype(BF16)

    def finish(layer, slabs, half):
        count = len(slabs)
        half = half + jnp.concatenate([bias_e[layer]] * count, axis=1)
        message = dot(mat_o[layer], silu_of_half(half).astype(BF16))
        weighted = []
        for index, (x, d) in enumerate(slabs):
            own = message[:, index * cz : (index + 1) * cz]
            e_s[d, x] = (e_s[d, x].astype(F32) + own).astype(BF16)
            weighted.append(w_s[d, x][None] * own.reshape(chans, cy, cz))
        return weighted

    def edges_xz(layer, slabs):
        nothing = jnp.zeros((rows, cz), BF16)
        own = jnp.concatenate([h_s[x] for x, d in slabs], axis=1)
        other = jnp.concatenate(
            [hz_s[x] if d == 2 else h_s[x + 1] if x < last else nothing for x, d in slabs], axis=1
        )
        edge = jnp.concatenate([e_s[d, x] for x, d in slabs], axis=1)
        stacked = jnp.concatenate([own, other, edge], axis=0)
        return finish(layer, slabs, dot(mat_e[layer, :, 0 : 3 * rows], stacked))

    def edges_y(layer, xs):
        edge = jnp.concatenate([e_s[1, x] for x in xs], axis=1)
        own = jnp.concatenate([h_s[x] for x in xs], axis=1)
        stacked = jnp.concatenate([edge, own], axis=0)
        slabs = [(x, 1) for x in xs]
        return finish(layer, slabs, dot(mat_e[layer, :, 2 * rows :], stacked))

    def both_y(weighted):
        return weighted + pltpu.roll(weighted, 1, 1)

    def both_z(weighted):
        return weighted + pltpu.roll(weighted, 1, 2)

    def put(slot, x, value, add):
        value = value.reshape(rows, cz)
        if add:
            value = p_s[slot, x] + value
        p_s[slot, x] = value

    def transfer(way, slot):
        dx, dy, dz = way
        side = 0 if dy < 0 else 1
        face = 0 if dx < 0 else last
        if dz != 0:
            source = zsend.at[slot, 0 if dz < 0 else 1]
            target = zrx.at[slot, (dx + 1) * 6 + (dy + 1) * 2 + (0 if dz < 0 else 1)]
        elif dy == 0:
            source = p_s.at[slot, face]
            target = xrx.at[slot, 0 if dx < 0 else 1]
        elif dx == 0:
            source = ysend.at[slot, side]
            target = yrx.at[slot, side]
        else:
            source = ysend.at[slot, side, face]
            target = xyrx.at[slot, (0 if dx < 0 else 2) + side]
        index = WAYS.index(way)
        return pltpu.make_async_remote_copy(
            src_ref=source,
            dst_ref=target,
            send_sem=send_sem.at[slot, index],
            recv_sem=recv_sem.at[slot, index],
            device_id=device(way),
            device_id_type=MESH,
        )

    def start(way, slot):
        @pl.when(exists(way))
        def _():
            transfer(way, slot).start()

    def arrive(way, slot):
        @pl.when(exists(back(way)))
        def _():
            transfer(way, slot).wait_recv()

    def sent(way, slot):
        @pl.when(exists(way))
        def _():
            transfer(way, slot).wait_send()

    x_ways = [way for way in ways if way[1] == 0 and way[2] == 0]
    y_ways = [way for way in ways if way[1] != 0 and way[2] == 0]
    z_ways = [way for way in ways if way[2] != 0]

    z_row, z_lane = iota((2 * zrows, 128), 0), iota((2 * zrows, 128), 1)

    def z_faces(slot):
        faces = jnp.zeros((2 * zrows, 128), F32)
        for x in range(cx):
            for part in range(halves):
                high, low = split(p_s[slot, x, part * 128 : (part + 1) * 128])
                at = x * halves + part
                pick = ((z_row == at) & (z_lane == 0)) | (
                    (z_row == zrows + at) & (z_lane == cz - 1)
                )
                pick = pick.astype(F32).astype(BF16)
                for piece in (high, low):
                    faces = faces + lax.dot_general(
                        pick, piece, (((1,), (1,)), ((), ())), preferred_element_type=F32
                    )
        zsend[slot, 0] = faces[:zrows]
        zsend[slot, 1] = faces[zrows:]

    row_z, lane_z = iota((zrows, 128), 0), iota((zrows, 128), 1)

    def z_total(slot, dz):
        total = jnp.zeros((zrows, 128), F32)
        shift_x, shift_y = last * halves, cy - 1
        for dy in (-1, 0, 1):
            part = jnp.zeros((zrows, 128), F32)
            for dx in (-1, 0, 1):
                piece = zrx[slot, (dx + 1) * 6 + (dy + 1) * 2 + (0 if dz < 0 else 1)]
                if dx > 0:
                    piece = jnp.where(row_z < halves, pltpu.roll(piece, zrows - shift_x, 0), 0.0)
                if dx < 0:
                    inside = (row_z >= shift_x) & (row_z < shift_x + halves)
                    piece = jnp.where(inside, pltpu.roll(piece, shift_x, 0), 0.0)
                part = part + piece
            if dy > 0:
                part = jnp.where(lane_z % cy == 0, pltpu.roll(part, 128 - shift_y, 1), 0.0)
            if dy < 0:
                part = jnp.where(lane_z % cy == cy - 1, pltpu.roll(part, shift_y, 1), 0.0)
            total = total + part
        return total

    def z_columns(slot):
        both = jnp.concatenate(
            [z_total(slot, 1), z_total(slot, -1), jnp.zeros((128 - 2 * zrows, 128), F32)], axis=0
        )
        high, low = split(both.T)
        return jnp.concatenate([high, low], axis=1)

    place_row, place_lane = iota((256, cz), 0) % 128, iota((256, cz), 1)

    def z_add(columns, x):
        out = []
        for part in range(halves):
            at = x * halves + part
            pick = ((place_row == at) & (place_lane == 0)) | (
                (place_row == zrows + at) & (place_lane == cz - 1)
            )
            out.append(dot(columns, pick.astype(F32).astype(BF16)))
        return jnp.concatenate(out, axis=0)

    def y_rows(side):
        return pl.ds(0 if side == 0 else cy - 1, chans, stride=cy)

    def node(layer, slot, x, columns):
        total = p_s[slot, x] + z_add(columns, x)
        if x == 0:
            total = total + xrx[slot, 1]
        if x == last:
            total = total + xrx[slot, 0]
        inc_s[x] = total
        for side in range(2):
            extra = yrx[slot, 1 - side, x]
            if x == 0:
                extra = extra + xyrx[slot, 2 + (1 - side)]
            if x == last:
                extra = extra + xyrx[slot, 1 - side]
            inc_s[x, y_rows(side), :] = inc_s[x, y_rows(side), :] + extra
        stacked = jnp.concatenate([h_s[x], inc_s[x].astype(BF16)], axis=0)
        half = dot(mat_n[layer], stacked) + bias_n[layer]
        step = dot(mat_no[layer], silu_of_half(half).astype(BF16))
        return (h_s[x].astype(F32) + step).astype(BF16).astype(F32)

    middle = list(range(1, last))

    def middle_edges(layer, slot):
        for x in middle:
            (wz,) = edges_xz(layer, [(x, 2)])
            (wy,) = edges_y(layer, [x])
            put(slot, x, both_z(wz) + both_y(wy), False)

    middle_edges(0, 0)
    pl.semaphore_wait(
        barrier,
        functools.reduce(
            lambda a, b: a * b,
            [
                1 + (pos > 0).astype(jnp.int32) + (pos < size - 1).astype(jnp.int32)
                for pos, size in zip(place, sizes)
            ],
        )
        - 1,
    )

    def layer_step(layer, carry):
        slot = lax.rem(layer, slots)
        after = lax.rem(layer + 1, slots)
        w0, wz = edges_xz(layer, [(0, 0), (0, 2)])
        (wy,) = edges_y(layer, [0])
        put(slot, 0, w0 + both_z(wz) + both_y(wy), False)
        for way in x_ways:
            if way[0] < 0:
                start(way, slot)
        ring = [(x, 0) for x in range(1, cx)]
        *wx, wz = edges_xz(layer, ring + [(last, 2)])
        (wy,) = edges_y(layer, [last])
        wx = [w0] + wx
        put(slot, last, wx[last - 1] + wx[last] + both_z(wz) + both_y(wy), False)
        for way in x_ways:
            if way[0] > 0:
                start(way, slot)
        for x in middle:
            put(slot, x, wx[x - 1] + wx[x], True)
        for side in range(2):
            for x in range(cx):
                ysend[slot, side, x] = p_s[slot, x, y_rows(side), :]
        for way in y_ways:
            start(way, slot)
        z_faces(slot)
        for way in z_ways:
            start(way, slot)
        for way in y_ways + z_ways:
            arrive(way, slot)
        columns = z_columns(slot)
        for x in middle:
            keep_nodes(x, node(layer, slot, x, columns))

        @pl.when(layer + 1 < layers)
        def _():
            middle_edges(layer + 1, after)

        for way in x_ways:
            arrive(way, slot)
        keep_nodes(0, node(layer, slot, 0, columns))
        keep_nodes(last, node(layer, slot, last, columns))
        for way in ways:
            sent(way, slot)
        return carry

    lax.fori_loop(0, layers, layer_step, 0)
    for x in range(cx):
        out_ref[:, x] = h_s[x].astype(F32).reshape(chans, cy, cz).astype(BF16)


def solution(mesh):
    sizes = tuple(mesh.shape[axis] for axis in AXES)

    def on_device(features, edge_state, multiplicity, *params):
        layers = params[0].shape[0]
        chans, cx, cy, cz = features.shape
        rows = chans * cy
        assert cz == 128 and rows % 128 == 0 and cy % 8 == 0 and cx > 1
        slots = min(layers, 2)
        zrows = -(-cx * (rows // 128) // 8) * 8
        vmem = pl.BlockSpec(memory_space=pltpu.VMEM)
        scratch = [
            pltpu.VMEM((cx, rows, cz), BF16),
            pltpu.VMEM((cx, rows, cz), BF16),
            pltpu.VMEM((3, cx, rows, cz), BF16),
            pltpu.VMEM((3, cx, cy, cz), F32),
            pltpu.VMEM((slots, cx, rows, cz), F32),
            pltpu.VMEM((cx, rows, cz), F32),
            pltpu.VMEM((layers, rows, 4 * rows), BF16),
            pltpu.VMEM((layers, rows, rows), BF16),
            pltpu.VMEM((layers, rows, 2 * rows), BF16),
            pltpu.VMEM((layers, rows, rows), BF16),
            pltpu.VMEM((layers, rows, cz), F32),
            pltpu.VMEM((layers, rows, cz), F32),
            pltpu.VMEM((slots, 2, cx, chans, cz), F32),
            pltpu.VMEM((slots, 2, zrows, 128), F32),
            pltpu.VMEM((slots, 2, rows, cz), F32),
            pltpu.VMEM((slots, 2, cx, chans, cz), F32),
            pltpu.VMEM((slots, 4, chans, cz), F32),
            pltpu.VMEM((slots, 18, zrows, 128), F32),
            pltpu.SemaphoreType.DMA((slots, len(WAYS))),
            pltpu.SemaphoreType.DMA((slots, len(WAYS))),
        ]
        return pl.pallas_call(
            functools.partial(kernel, sizes, layers),
            out_shape=jax.ShapeDtypeStruct(features.shape, features.dtype),
            in_specs=[vmem] * 9,
            out_specs=vmem,
            scratch_shapes=scratch,
            compiler_params=pltpu.CompilerParams(
                collective_id=0, has_side_effects=True, vmem_limit_bytes=48 * 1024 * 1024
            ),
        )(features, edge_state, multiplicity, *params)

    placed = (P(None, *AXES), P(None, None, *AXES), P(*AXES)) + (P(),) * 6
    return jax.shard_map(
        on_device, mesh=mesh, in_specs=placed, out_specs=P(None, *AXES), check_vma=False
    )
```

time: 137 us -> 41.7 us (0.30)
  the two profiles are of different devices: /device:TPU:24 before, /device:TPU:1 now
where the time goes in v1:
time: 41.7 us; the launch traced here: 41.2 us
  Pallas kernels  33.5 us (80%)
  local copies, waits for them, and re-layouts  7.69 us (18%)
    pallas_call x1, Pallas kernels, on_device(): pl.pallas_call(functools.partial(kernel, sizes, layers), out_shape=jax.Sh...  33.5 us
    unnamed x19, local copies, waits for them, and re-layouts  7.69 us

profile of v1, /device:TPU:1, one launch (start us, length us, event | category | flops | bytes accessed | tf_op | source)
XLA Modules:
  0.0 41.2 jit_solution(1690372223062333711)
XLA Ops:
  0.0 0.0 copy-start
  0.0 1.1 %copy-done = bf16[3,32,3,8,128]{4,3,2,1,0:T(8,128)(2,1)S(1)} copy-done((bf16[3,32,3,8,128]{4,3,2,1,0:T(8,128)(2,1)S(1)}, bf16[3,32,3,8,128]{4,3,2,1,0:T(8,128)(2,1)}, u32[]{:S(2)}) %copy-start) | copy-done | bytes 589848
  1.1 0.0 copy-start.1
  1.1 0.9 %copy-done.1 = bf16[32,3,8,128]{3,2,1,0:T(8,128)(2,1)S(1)} copy-done((bf16[32,3,8,128]{3,2,1,0:T(8,128)(2,1)S(1)}, bf16[32,3,8,128]{3,2,1,0:T(8,128)(2,1)}, u32[]{:S(2)}) %copy-start.1) | copy-done | bytes 196632
  2.0 0.0 copy-start.2
  2.0 0.7 %copy-done.2 = bf16[3,32,96]{2,1,0:T(8,128)(2,1)S(1)} copy-done((bf16[3,32,96]{2,1,0:T(8,128)(2,1)S(1)}, bf16[3,32,96]{2,1,0:T(8,128)(2,1)}, u32[]{:S(2)}) %copy-start.2) | copy-done | bytes 18456
  2.7 0.0 copy-start.3
  2.7 0.7 %copy-done.3 = bf16[3,32,32]{2,1,0:T(8,128)(2,1)S(1)} copy-done((bf16[3,32,32]{2,1,0:T(8,128)(2,1)S(1)}, bf16[3,32,32]{2,1,0:T(8,128)(2,1)}, u32[]{:S(2)}) %copy-start.3) | copy-done | bytes 6168
  3.5 0.0 copy-start.4
  3.5 0.7 %copy-done.4 = bf16[3,32,64]{2,1,0:T(8,128)(2,1)S(1)} copy-done((bf16[3,32,64]{2,1,0:T(8,128)(2,1)S(1)}, bf16[3,32,64]{2,1,0:T(8,128)(2,1)}, u32[]{:S(2)}) %copy-start.4) | copy-done | bytes 12312
  4.2 0.0 copy-start.5
  4.2 0.7 %copy-done.5 = bf16[3,32,32]{2,1,0:T(8,128)(2,1)S(1)} copy-done((bf16[3,32,32]{2,1,0:T(8,128)(2,1)S(1)}, bf16[3,32,32]{2,1,0:T(8,128)(2,1)}, u32[]{:S(2)}) %copy-start.5) | copy-done | bytes 6168
  4.9 0.0 copy-start.6
  4.9 0.7 %copy-done.6 = s32[3,8,128]{2,1,0:T(8,128)S(1)} copy-done((s32[3,8,128]{2,1,0:T(8,128)S(1)}, s32[3,8,128]{2,1,0:T(8,128)}, u32[]{:S(2)}) %copy-start.6) | copy-done | bytes 12312
  5.7 0.0 copy-start.7
  5.7 0.7 %copy-done.7 = f32[3,32]{1,0:T(4,128)S(1)} copy-done((f32[3,32]{1,0:T(4,128)S(1)}, f32[3,32]{1,0:T(4,128)}, u32[]{:S(2)}) %copy-start.7) | copy-done | bytes 408
  6.3 0.0 copy-start.8
  6.3 0.7 %copy-done.8 = f32[3,32]{1,0:T(4,128)S(1)} copy-done((f32[3,32]{1,0:T(4,128)S(1)}, f32[3,32]{1,0:T(4,128)}, u32[]{:S(2)}) %copy-start.8) | copy-done | bytes 408
  7.0 33.5 %shard_map.91 = bf16[32,3,8,128]{3,2,1,0:T(8,128)(2,1)S(1)} custom-call(bf16[32,3,8,128]{3,2,1,0:T(8,128)(2,1)S(1)} %copy-done.1, bf16[3,32,3,8,128]{4,3,2,1,0:T(8,128)(2,1)S(1)} %copy-done, s32[3,8,128]{2,1,0:T(8,128)S(1)} %copy-done.6, bf16[3,32,96]{2,1,0:T(8,128)(2,1)S(1)} %copy-done.2, bf16[3,32,32]{2,1,0:T(8,128)(2,1)S(1)} %copy-done.3, ...), custom_call_target="tpu_custom_call" | custom-call | tf_op jit(solution)/shard_map/pallas_call | solution.py:414
  40.5 0.7 %copy.11 = bf16[32,3,8,128]{3,2,1,0:T(8,128)(2,1)} copy(bf16[32,3,8,128]{3,2,1,0:T(8,128)(2,1)S(1)} %shard_map.91) | data formatting | bytes 393216
Async XLA Ops:
  0.0 1.1 %copy-start = (bf16[3,32,3,8,128]{4,3,2,1,0:T(8,128)(2,1)S(1)}, bf16[3,32,3,8,128]{4,3,2,1,0:T(8,128)(2,1)}, u32[]{:S(2)}) copy-start(bf16[3,32,3,8,128]{4,3,2,1,0:T(8,128)(2,1)} %edge_ref.1) | copy-start | bytes 1769476
  1.1 0.9 %copy-start.1 = (bf16[32,3,8,128]{3,2,1,0:T(8,128)(2,1)S(1)}, bf16[32,3,8,128]{3,2,1,0:T(8,128)(2,1)}, u32[]{:S(2)}) copy-start(bf16[32,3,8,128]{3,2,1,0:T(8,128)(2,1)} %feat_ref.1) | copy-start | bytes 589828
  2.0 0.7 %copy-start.2 = (bf16[3,32,96]{2,1,0:T(8,128)(2,1)S(1)}, bf16[3,32,96]{2,1,0:T(8,128)(2,1)}, u32[]{:S(2)}) copy-start(bf16[3,32,96]{2,1,0:T(8,128)(2,1)} %win_ref.1) | copy-start | bytes 55300
  2.7 0.7 %copy-start.3 = (bf16[3,32,32]{2,1,0:T(8,128)(2,1)S(1)}, bf16[3,32,32]{2,1,0:T(8,128)(2,1)}, u32[]{:S(2)}) copy-start(bf16[3,32,32]{2,1,0:T(8,128)(2,1)} %wout_ref.1) | copy-start | bytes 18436
  3.5 0.7 %copy-start.4 = (bf16[3,32,64]{2,1,0:T(8,128)(2,1)S(1)}, bf16[3,32,64]{2,1,0:T(8,128)(2,1)}, u32[]{:S(2)}) copy-start(bf16[3,32,64]{2,1,0:T(8,128)(2,1)} %nin_ref.1) | copy-start | bytes 36868
  4.2 0.7 %copy-start.5 = (bf16[3,32,32]{2,1,0:T(8,128)(2,1)S(1)}, bf16[3,32,32]{2,1,0:T(8,128)(2,1)}, u32[]{:S(2)}) copy-start(bf16[3,32,32]{2,1,0:T(8,128)(2,1)} %nout_ref.1) | copy-start | bytes 18436
  4.9 0.7 %copy-start.6 = (s32[3,8,128]{2,1,0:T(8,128)S(1)}, s32[3,8,128]{2,1,0:T(8,128)}, u32[]{:S(2)}) copy-start(s32[3,8,128]{2,1,0:T(8,128)} %mult_ref.1) | copy-start | bytes 36868
  5.7 0.7 %copy-start.7 = (f32[3,32]{1,0:T(4,128)S(1)}, f32[3,32]{1,0:T(4,128)}, u32[]{:S(2)}) copy-start(f32[3,32]{1,0:T(4,128)} %bin_ref.1) | copy-start | bytes 1156
  6.3 0.7 %copy-start.8 = (f32[3,32]{1,0:T(4,128)S(1)}, f32[3,32]{1,0:T(4,128)}, u32[]{:S(2)}) copy-start(f32[3,32]{1,0:T(4,128)} %bnode_ref.1) | copy-start | bytes 1156

commit v2 on v1

--- a/solution.py
+++ b/solution.py
@@ -11,7 +11,8 @@
 MESH = pl.DeviceIdType.MESH
 AXES = ("gx", "gy", "gz")
 F32, BF16 = jnp.float32, jnp.bfloat16
-WAYS = [way for way in itertools.product((-1, 0, 1), repeat=3) if any(way)]
+STEPS = (-1, 0, 1)
+OTHER = 2
 
 
 def iota(shape, dim):
@@ -26,43 +27,68 @@
     return half + half * jnp.tanh(half)
 
 
-def split(values):
-    high = values.astype(BF16)
-    return high, (values - high.astype(F32)).astype(BF16)
+def ways_of(sizes):
+    z_steps = {1: (0,), 2: (0, OTHER)}.get(sizes[2], STEPS)
+    ways = itertools.product(STEPS, STEPS, z_steps)
+    return [
+        way for way in ways if any(way) and all(s == 0 or n > 1 for s, n in zip(way, sizes))
+    ]
 
 
 def kernel(
     sizes,
     layers,
+    feat_hbm, edge_hbm, mult_hbm, win_hbm, wout_hbm, bin_hbm, nin_hbm, nout_hbm, bnode_hbm,
+    out_ref,
     feat_ref, edge_ref, mult_ref, win_ref, wout_ref, bin_ref, nin_ref, nout_ref, bnode_ref,
-    out_ref,
     h_s, hz_s, e_s, w_s, p_s, inc_s, mat_e, mat_o, mat_n, mat_no, bias_e, bias_n,
-    ysend, zsend, xrx, yrx, xyrx, zrx, send_sem, recv_sem,
+    ysend, zsend, xrx, yrx, xyrx, zrx, turn_s, in_sem, send_sem, recv_sem,
 ):
+    loads = [
+        pltpu.make_async_copy(source, target, in_sem.at[index])
+        for index, (source, target) in enumerate([
+            (win_hbm, win_ref), (wout_hbm, wout_ref), (bin_hbm, bin_ref), (nin_hbm, nin_ref),
+            (nout_hbm, nout_ref), (bnode_hbm, bnode_ref), (mult_hbm, mult_ref),
+            (feat_hbm, feat_ref), (edge_hbm, edge_ref),
+        ])
+    ]
+    for load in loads:
+        load.start()
+
     chans, cx, cy, cz = feat_ref.shape
     rows = chans * cy
     halves = rows // 128
     last = cx - 1
-    slots = p_s.shape[0]
     zrows = zsend.shape[2]
     place = [lax.axis_index(axis) for axis in AXES]
 
     def exists(way):
         there = None
         for pos, step, size in zip(place, way, sizes):
-            if step == 0:
+            if step == 0 or step == OTHER:
                 continue
             here = pos > 0 if step < 0 else pos < size - 1
             there = here if there is None else there & here
         return there
 
     def device(way):
-        return {axis: pos + step for axis, pos, step in zip(AXES, place, way)}
+        return {
+            axis: 1 - pos if step == OTHER else pos + step
+            for axis, pos, step in zip(AXES, place, way)
+        }
 
     def back(way):
-        return tuple(-step for step in way)
-
-    ways = [way for way in WAYS if all(step == 0 or size > 1 for step, size in zip(way, sizes))]
+        return tuple(step if step == OTHER else -step for step in way)
+
+    def when_exists(way, act):
+        there = exists(way)
+        if there is None:
+            act()
+        else:
+            pl.when(there)(act)
+
+    ways = ways_of(sizes)
+    z_steps = [way[2] for way in ways if way[0] == 0 and way[1] == 0 and way[2] != 0]
 
     xrx[...] = jnp.zeros_like(xrx)
     yrx[...] = jnp.zeros_like(yrx)
@@ -71,48 +97,57 @@
 
     barrier = pltpu.get_barrier_semaphore()
     for way in ways:
-        @pl.when(exists(way))
-        def _():
+        def greet(way=way):
             pl.semaphore_signal(barrier, inc=1, device_id=device(way), device_id_type=MESH)
 
-    spread = (iota((rows, chans), 0) // cy == iota((rows, chans), 1)).astype(F32).astype(BF16)
-    row_y, col_y = iota((rows, rows), 0) % cy, iota((rows, rows), 1) % cy
-    same_y, next_y = row_y == col_y, row_y + 1 == col_y
-
-    def widen(tall, part):
-        width = tall.shape[1]
-        pick = iota((width, rows), 0) == part * chans + iota((width, rows), 1) // cy
-        return dot(tall, pick.astype(F32).astype(BF16))
+        when_exists(way, greet)
+
+    mine = iota((rows, chans), 0) // cy == iota((rows, chans), 1)
+    spread = mine.astype(F32).astype(BF16)
+    row_y, col_y = iota((cy, rows), 0), iota((cy, rows), 1) % cy
+    same_y = (row_y == col_y).astype(F32)
+    half_same, half_next = 0.5 * same_y, 0.5 * (row_y + 1 == col_y).astype(F32)
+    col_c = iota((1, rows), 1) // cy
+
+    def widen(weights):
+        width = weights.shape[1]
+        parts = []
+        for part in range(width // chans):
+            pick = iota((width, rows), 0) == part * chans + col_c
+            parts.append(dot(weights, pick.astype(F32).astype(BF16)).astype(BF16))
+        return parts
 
     def build(layer):
-        tall = dot(spread, win_ref[layer]).astype(BF16)
-        own, other, edge = (0.5 * widen(tall, part) for part in range(3))
-        own = jnp.where(same_y, own, 0.0)
-        mat_e[layer, :, 0:rows] = own.astype(BF16)
-        mat_e[layer, :, rows : 2 * rows] = jnp.where(same_y, other, 0.0).astype(BF16)
-        mat_e[layer, :, 2 * rows : 3 * rows] = jnp.where(same_y, edge, 0.0).astype(BF16)
-        mat_e[layer, :, 3 * rows :] = jnp.where(next_y, other, own).astype(BF16)
-        tall = dot(spread, wout_ref[layer]).astype(BF16)
-        mat_o[layer] = jnp.where(same_y, widen(tall, 0), 0.0).astype(BF16)
-        tall = dot(spread, nin_ref[layer]).astype(BF16)
-        for part in range(2):
-            mat_n[layer, :, part * rows : (part + 1) * rows] = jnp.where(
-                same_y, 0.5 * widen(tall, part), 0.0
-            ).astype(BF16)
-        tall = dot(spread, nout_ref[layer]).astype(BF16)
-        mat_no[layer] = jnp.where(same_y, widen(tall, 0), 0.0).astype(BF16)
-        mine = iota((rows, chans), 0) // cy == iota((rows, chans), 1)
+        wide = widen(win_ref[layer]) + widen(wout_ref[layer])
+        wide += widen(nin_ref[layer]) + widen(nout_ref[layer])
+
+        def block(index):
+            return dot(spread, wide[index]).reshape(chans, cy, rows)
+
+        def flat(values):
+            return values.reshape(rows, rows).astype(BF16)
+
+        own, other = block(0), block(1)
+        own_same = own * half_same[None]
+        mat_e[layer, :, 0:rows] = flat(own_same)
+        mat_e[layer, :, rows : 2 * rows] = flat(other * half_same[None])
+        mat_e[layer, :, 2 * rows : 3 * rows] = flat(block(2) * half_same[None])
+        mat_e[layer, :, 3 * rows :] = flat(own_same + other * half_next[None])
+        mat_o[layer] = flat(block(3) * same_y[None])
+        mat_n[layer, :, 0:rows] = flat(block(4) * half_same[None])
+        mat_n[layer, :, rows:] = flat(block(5) * half_same[None])
+        mat_no[layer] = flat(block(6) * same_y[None])
         for source, target in ((bin_ref, bias_e), (bnode_ref, bias_n)):
             column = jnp.sum(
                 jnp.where(mine, source[pl.ds(layer, 1), :], 0.0), axis=1, keepdims=True
             )
             target[layer] = jnp.broadcast_to(0.5 * column, (rows, cz))
 
-    def build_step(layer, carry):
-        build(layer)
-        return carry
-
-    lax.fori_loop(0, layers, build_step, 0)
+    for load in loads[:6]:
+        load.wait()
+    build(0)
+    for load in loads[6:]:
+        load.wait()
 
     fluid = mult_ref[1, 1:2, 1:2] > 0
     zeros = jnp.zeros((cy, cz), jnp.int32)
@@ -182,11 +217,13 @@
 
     def transfer(way, slot):
         dx, dy, dz = way
+        index = ways.index(way)
         side = 0 if dy < 0 else 1
         face = 0 if dx < 0 else last
         if dz != 0:
-            source = zsend.at[slot, 0 if dz < 0 else 1]
-            target = zrx.at[slot, (dx + 1) * 6 + (dy + 1) * 2 + (0 if dz < 0 else 1)]
+            which = z_steps.index(dz)
+            source = zsend.at[slot, which]
+            target = zrx.at[slot, which, (dx + 1) * 3 + dy + 1]
         elif dy == 0:
             source = p_s.at[slot, face]
             target = xrx.at[slot, 0 if dx < 0 else 1]
@@ -196,7 +233,6 @@
         else:
             source = ysend.at[slot, side, face]
             target = xyrx.at[slot, (0 if dx < 0 else 2) + side]
-        index = WAYS.index(way)
         return pltpu.make_async_remote_copy(
             src_ref=source,
             dst_ref=target,
@@ -207,52 +243,45 @@
         )
 
     def start(way, slot):
-        @pl.when(exists(way))
-        def _():
-            transfer(way, slot).start()
+        when_exists(way, lambda: transfer(way, slot).start())
 
     def arrive(way, slot):
-        @pl.when(exists(back(way)))
-        def _():
-            transfer(way, slot).wait_recv()
+        when_exists(back(way), lambda: transfer(way, slot).wait_recv())
 
     def sent(way, slot):
-        @pl.when(exists(way))
-        def _():
-            transfer(way, slot).wait_send()
+        when_exists(way, lambda: transfer(way, slot).wait_send())
 
     x_ways = [way for way in ways if way[1] == 0 and way[2] == 0]
     y_ways = [way for way in ways if way[1] != 0 and way[2] == 0]
     z_ways = [way for way in ways if way[2] != 0]
 
-    z_row, z_lane = iota((2 * zrows, 128), 0), iota((2 * zrows, 128), 1)
+    lane = iota((128, cz), 1)
+    odd_rows, even_rows = pl.ds(1, zrows, stride=2), pl.ds(0, zrows, stride=2)
 
     def z_faces(slot):
-        faces = jnp.zeros((2 * zrows, 128), F32)
+        faces = jnp.zeros((128, cz), F32)
         for x in range(cx):
             for part in range(halves):
-                high, low = split(p_s[slot, x, part * 128 : (part + 1) * 128])
-                at = x * halves + part
-                pick = ((z_row == at) & (z_lane == 0)) | (
-                    (z_row == zrows + at) & (z_lane == cz - 1)
-                )
-                pick = pick.astype(F32).astype(BF16)
-                for piece in (high, low):
-                    faces = faces + lax.dot_general(
-                        pick, piece, (((1,), (1,)), ((), ())), preferred_element_type=F32
-                    )
-        zsend[slot, 0] = faces[:zrows]
-        zsend[slot, 1] = faces[zrows:]
+                at = 2 * (x * halves + part)
+                piece = pltpu.roll(p_s[slot, x, part * 128 : (part + 1) * 128], at + 1, 1)
+                faces = jnp.where((lane == at) | (lane == at + 1), piece, faces)
+        turn_s[0] = faces.T
+        first, final = turn_s[0, odd_rows, :], turn_s[0, even_rows, :]
+        for which, dz in enumerate(z_steps):
+            if dz == OTHER:
+                zsend[slot, which] = jnp.where(place[2] == 0, final, first)
+            else:
+                zsend[slot, which] = first if dz < 0 else final
 
     row_z, lane_z = iota((zrows, 128), 0), iota((zrows, 128), 1)
 
-    def z_total(slot, dz):
+    def z_total(slot, which):
         total = jnp.zeros((zrows, 128), F32)
         shift_x, shift_y = last * halves, cy - 1
         for dy in (-1, 0, 1):
             part = jnp.zeros((zrows, 128), F32)
             for dx in (-1, 0, 1):
-                piece = zrx[slot, (dx + 1) * 6 + (dy + 1) * 2 + (0 if dz < 0 else 1)]
+                piece = zrx[slot, which, (dx + 1) * 3 + dy + 1]
                 if dx > 0:
                     piece = jnp.where(row_z < halves, pltpu.roll(piece, zrows - shift_x, 0), 0.0)
                 if dx < 0:
@@ -267,22 +296,20 @@
         return total
 
     def z_columns(slot):
-        both = jnp.concatenate(
-            [z_total(slot, 1), z_total(slot, -1), jnp.zeros((128 - 2 * zrows, 128), F32)], axis=0
-        )
-        high, low = split(both.T)
-        return jnp.concatenate([high, low], axis=1)
-
-    place_row, place_lane = iota((256, cz), 0) % 128, iota((256, cz), 1)
+        for which, dz in enumerate(z_steps):
+            total = z_total(slot, which)
+            if dz != 1:
+                turn_s[1, even_rows, :] = jnp.where(place[2] < sizes[2] - 1, total, 0.0)
+            if dz != -1:
+                turn_s[1, odd_rows, :] = jnp.where(place[2] > 0, total, 0.0)
+        return turn_s[1].T
 
     def z_add(columns, x):
         out = []
         for part in range(halves):
-            at = x * halves + part
-            pick = ((place_row == at) & (place_lane == 0)) | (
-                (place_row == zrows + at) & (place_lane == cz - 1)
-            )
-            out.append(dot(columns, pick.astype(F32).astype(BF16)))
+            at = 2 * (x * halves + part)
+            piece = pltpu.roll(columns, cz - at - 1, 1)
+            out.append(jnp.where((lane == 0) | (lane == cz - 1), piece, 0.0))
         return jnp.concatenate(out, axis=0)
 
     def y_rows(side):
@@ -315,25 +342,26 @@
             (wy,) = edges_y(layer, [x])
             put(slot, x, both_z(wz) + both_y(wy), False)
 
+    turn_s[1] = jnp.zeros_like(turn_s[1])
     middle_edges(0, 0)
-    pl.semaphore_wait(
-        barrier,
-        functools.reduce(
-            lambda a, b: a * b,
-            [
-                1 + (pos > 0).astype(jnp.int32) + (pos < size - 1).astype(jnp.int32)
-                for pos, size in zip(place, sizes)
-            ],
-        )
-        - 1,
+    greetings = -1 + functools.reduce(
+        lambda a, b: a * b,
+        [
+            1 + (pos > 0).astype(jnp.int32) + (pos < size - 1).astype(jnp.int32)
+            for pos, size in zip(place, sizes)
+        ],
     )
 
     def layer_step(layer, carry):
-        slot = lax.rem(layer, slots)
-        after = lax.rem(layer + 1, slots)
+        slot = layer
         w0, wz = edges_xz(layer, [(0, 0), (0, 2)])
         (wy,) = edges_y(layer, [0])
         put(slot, 0, w0 + both_z(wz) + both_y(wy), False)
+
+        @pl.when(layer == 0)
+        def _():
+            pl.semaphore_wait(barrier, greetings)
+
         for way in x_ways:
             if way[0] < 0:
                 start(way, slot)
@@ -355,6 +383,11 @@
         z_faces(slot)
         for way in z_ways:
             start(way, slot)
+
+        @pl.when(layer + 1 < layers)
+        def _():
+            build(layer + 1)
+
         for way in y_ways + z_ways:
             arrive(way, slot)
         columns = z_columns(slot)
@@ -363,17 +396,21 @@
 
         @pl.when(layer + 1 < layers)
         def _():
-            middle_edges(layer + 1, after)
+            middle_edges(layer + 1, layer + 1)
 
         for way in x_ways:
             arrive(way, slot)
         keep_nodes(0, node(layer, slot, 0, columns))
         keep_nodes(last, node(layer, slot, last, columns))
+        return carry
+
+    def sent_step(layer, carry):
         for way in ways:
-            sent(way, slot)
+            sent(way, layer)
         return carry
 
     lax.fori_loop(0, layers, layer_step, 0)
+    lax.fori_loop(0, layers, sent_step, 0)
     for x in range(cx):
         out_ref[:, x] = h_s[x].astype(F32).reshape(chans, cy, cz).astype(BF16)
 
@@ -386,10 +423,12 @@
         chans, cx, cy, cz = features.shape
         rows = chans * cy
         assert cz == 128 and rows % 128 == 0 and cy % 8 == 0 and cx > 1
-        slots = min(layers, 2)
+        slots = layers
+        ways = len(ways_of(sizes))
         zrows = -(-cx * (rows // 128) // 8) * 8
         vmem = pl.BlockSpec(memory_space=pltpu.VMEM)
-        scratch = [
+        scratch = [pltpu.VMEM(a.shape, a.dtype) for a in (features, edge_state, multiplicity, *params)]
+        scratch += [
             pltpu.VMEM((cx, rows, cz), BF16),
             pltpu.VMEM((cx, rows, cz), BF16),
             pltpu.VMEM((3, cx, rows, cz), BF16),
@@ -407,18 +446,20 @@
             pltpu.VMEM((slots, 2, rows, cz), F32),
             pltpu.VMEM((slots, 2, cx, chans, cz), F32),
             pltpu.VMEM((slots, 4, chans, cz), F32),
-            pltpu.VMEM((slots, 18, zrows, 128), F32),
-            pltpu.SemaphoreType.DMA((slots, len(WAYS))),
-            pltpu.SemaphoreType.DMA((slots, len(WAYS))),
+            pltpu.VMEM((slots, 2, 9, zrows, 128), F32),
+            pltpu.VMEM((2, 128, 128), F32),
+            pltpu.SemaphoreType.DMA((9,)),
+            pltpu.SemaphoreType.DMA((slots, ways)),
+            pltpu.SemaphoreType.DMA((slots, ways)),
         ]
         return pl.pallas_call(
             functools.partial(kernel, sizes, layers),
             out_shape=jax.ShapeDtypeStruct(features.shape, features.dtype),
-            in_specs=[vmem] * 9,
+            in_specs=[pl.BlockSpec(memory_space=pltpu.HBM)] * 9,
             out_specs=vmem,
             scratch_shapes=scratch,
             compiler_params=pltpu.CompilerParams(
-                collective_id=0, has_side_effects=True, vmem_limit_bytes=48 * 1024 * 1024
+                collective_id=0, has_side_effects=True, vmem_limit_bytes=60 * 1024 * 1024
             ),
         )(features, edge_state, multiplicity, *params)
 

time: 41.7 us -> 34 us (0.82)
  local copies, waits for them, and re-layouts: 7.69 us -> 1.62 us
  Pallas kernels: 33.5 us -> 32.1 us
    unnamed x19 -> x1, local copies, waits for them, and re-layouts: 7.69 us -> 1.62 us
    pallas_call x1, Pallas kernels: 33.5 us -> 32.1 us  [on_device(): pl.pallas_call(functools.partial(kernel, sizes, layers), out_shape=jax.Sh...]
where the time goes in v2:
time: 34 us; the launch traced here: 33.8 us
  Pallas kernels  32.1 us (94%)
  local copies, waits for them, and re-layouts  1.62 us (5%)
    pallas_call x1, Pallas kernels, on_device(): pl.pallas_call(functools.partial(kernel, sizes, layers), out_shape=jax.Sh...  32.1 us
    unnamed x1, local copies, waits for them, and re-layouts  1.62 us

profile of v2, /device:TPU:1, one launch (start us, length us, event | category | flops | bytes accessed | tf_op | source)
XLA Modules:
  0.0 33.8 jit_solution(4329023880861131059)
XLA Ops:
  0.0 32.1 %shard_map.91 = bf16[32,3,8,128]{3,2,1,0:T(8,128)(2,1)} custom-call(bf16[32,3,8,128]{3,2,1,0:T(8,128)(2,1)} %feat_hbm.1, bf16[3,32,3,8,128]{4,3,2,1,0:T(8,128)(2,1)} %edge_hbm.1, s32[3,8,128]{2,1,0:T(8,128)} %mult_hbm.1, bf16[3,32,96]{2,1,0:T(8,128)(2,1)} %win_hbm.1, bf16[3,32,32]{2,1,0:T(8,128)(2,1)} %wout_hbm.1, f32[3,32]{1,0:T(4,128)} %bin_hbm.1, ...), custom_call_target="tpu_custom_call" | custom-call | tf_op jit(solution)/shard_map/pallas_call | solution.py:455
  32.2 1.6 %copy.11 = bf16[32,3,8,128]{3,2,1,0:T(8,128)(2,1)} copy(bf16[32,3,8,128]{3,2,1,0:T(8,128)(2,1)} %shard_map.91) | data formatting | bytes 393216

commit v3 on v2

--- a/solution.py
+++ b/solution.py
@@ -12,6 +12,7 @@
 AXES = ("gx", "gy", "gz")
 F32, BF16 = jnp.float32, jnp.bfloat16
 STEPS = (-1, 0, 1)
+FAST, SLOW = 0, 1
 OTHER = 2
 
 
@@ -33,6 +34,17 @@
     return [
         way for way in ways if any(way) and all(s == 0 or n > 1 for s, n in zip(way, sizes))
     ]
+
+
+def messages_of(sizes, cx):
+    out = []
+    for way in ways_of(sizes):
+        dx, dy, dz = way
+        tags = (None,)
+        if dx == 0:
+            tags = (FAST, SLOW) if dz != 0 else range(cx)
+        out += [(way, tag) for tag in tags]
+    return out
 
 
 def kernel(
@@ -59,7 +71,7 @@
     rows = chans * cy
     halves = rows // 128
     last = cx - 1
-    zrows = zsend.shape[2]
+    zrows = zsend.shape[3]
     place = [lax.axis_index(axis) for axis in AXES]
 
     def exists(way):
@@ -88,6 +100,7 @@
             pl.when(there)(act)
 
     ways = ways_of(sizes)
+    messages = messages_of(sizes, cx)
     z_steps = [way[2] for way in ways if way[0] == 0 and way[1] == 0 and way[2] != 0]
 
     xrx[...] = jnp.zeros_like(xrx)
@@ -215,21 +228,22 @@
             value = p_s[slot, x] + value
         p_s[slot, x] = value
 
-    def transfer(way, slot):
+    def transfer(message, slot, slow):
+        way, tag = message
         dx, dy, dz = way
-        index = ways.index(way)
+        index = messages.index(message)
         side = 0 if dy < 0 else 1
         face = 0 if dx < 0 else last
         if dz != 0:
             which = z_steps.index(dz)
-            source = zsend.at[slot, which]
-            target = zrx.at[slot, which, (dx + 1) * 3 + dy + 1]
+            source = zsend.at[slot, which, SLOW if tag is None and face == slow else tag or FAST]
+            target = zrx.at[slot, which, {-1: 0, 0: 1 + (tag or 0), 1: 3}[dx], dy + 1]
         elif dy == 0:
             source = p_s.at[slot, face]
             target = xrx.at[slot, 0 if dx < 0 else 1]
         elif dx == 0:
-            source = ysend.at[slot, side]
-            target = yrx.at[slot, side]
+            source = ysend.at[slot, side, tag]
+            target = yrx.at[slot, side, tag]
         else:
             source = ysend.at[slot, side, face]
             target = xyrx.at[slot, (0 if dx < 0 else 2) + side]
@@ -242,52 +256,48 @@
             device_id_type=MESH,
         )
 
-    def start(way, slot):
-        when_exists(way, lambda: transfer(way, slot).start())
-
-    def arrive(way, slot):
-        when_exists(back(way), lambda: transfer(way, slot).wait_recv())
-
-    def sent(way, slot):
-        when_exists(way, lambda: transfer(way, slot).wait_send())
-
-    x_ways = [way for way in ways if way[1] == 0 and way[2] == 0]
-    y_ways = [way for way in ways if way[1] != 0 and way[2] == 0]
-    z_ways = [way for way in ways if way[2] != 0]
+    def start(message, slot, slow):
+        when_exists(message[0], lambda: transfer(message, slot, slow).start())
+
+    def arrive(message, slot, slow):
+        when_exists(back(message[0]), lambda: transfer(message, slot, slow).wait_recv())
+
+    def sent(message, slot, slow):
+        when_exists(message[0], lambda: transfer(message, slot, slow).wait_send())
 
     lane = iota((128, cz), 1)
     odd_rows, even_rows = pl.ds(1, zrows, stride=2), pl.ds(0, zrows, stride=2)
 
-    def z_faces(slot):
+    def z_faces(slot, xs, phase):
         faces = jnp.zeros((128, cz), F32)
-        for x in range(cx):
+        for x in xs:
             for part in range(halves):
                 at = 2 * (x * halves + part)
                 piece = pltpu.roll(p_s[slot, x, part * 128 : (part + 1) * 128], at + 1, 1)
                 faces = jnp.where((lane == at) | (lane == at + 1), piece, faces)
-        turn_s[0] = faces.T
-        first, final = turn_s[0, odd_rows, :], turn_s[0, even_rows, :]
+        turn_s[2] = faces.T
+        first, final = turn_s[2, odd_rows, :], turn_s[2, even_rows, :]
         for which, dz in enumerate(z_steps):
             if dz == OTHER:
-                zsend[slot, which] = jnp.where(place[2] == 0, final, first)
+                zsend[slot, which, phase] = jnp.where(place[2] == 0, final, first)
             else:
-                zsend[slot, which] = first if dz < 0 else final
+                zsend[slot, which, phase] = first if dz < 0 else final
 
     row_z, lane_z = iota((zrows, 128), 0), iota((zrows, 128), 1)
 
-    def z_total(slot, which):
+    def z_total(slot, which, face, phase):
         total = jnp.zeros((zrows, 128), F32)
         shift_x, shift_y = last * halves, cy - 1
-        for dy in (-1, 0, 1):
-            part = jnp.zeros((zrows, 128), F32)
-            for dx in (-1, 0, 1):
-                piece = zrx[slot, which, (dx + 1) * 3 + dy + 1]
-                if dx > 0:
-                    piece = jnp.where(row_z < halves, pltpu.roll(piece, zrows - shift_x, 0), 0.0)
-                if dx < 0:
-                    inside = (row_z >= shift_x) & (row_z < shift_x + halves)
-                    piece = jnp.where(inside, pltpu.roll(piece, shift_x, 0), 0.0)
-                part = part + piece
+        for dy in STEPS:
+            part = zrx[slot, which, 1 + phase, dy + 1]
+            if face == 0:
+                piece = zrx[slot, which, 3, dy + 1]
+                piece = jnp.where(row_z < halves, pltpu.roll(piece, zrows - shift_x, 0), 0.0)
+            else:
+                piece = zrx[slot, which, 0, dy + 1]
+                inside = (row_z >= shift_x) & (row_z < shift_x + halves)
+                piece = jnp.where(inside, pltpu.roll(piece, shift_x, 0), 0.0)
+            part = part + piece
             if dy > 0:
                 part = jnp.where(lane_z % cy == 0, pltpu.roll(part, 128 - shift_y, 1), 0.0)
             if dy < 0:
@@ -295,14 +305,14 @@
             total = total + part
         return total
 
-    def z_columns(slot):
+    def z_columns(slot, face, phase):
         for which, dz in enumerate(z_steps):
-            total = z_total(slot, which)
+            total = z_total(slot, which, face, phase)
             if dz != 1:
-                turn_s[1, even_rows, :] = jnp.where(place[2] < sizes[2] - 1, total, 0.0)
+                turn_s[phase, even_rows, :] = jnp.where(place[2] < sizes[2] - 1, total, 0.0)
             if dz != -1:
-                turn_s[1, odd_rows, :] = jnp.where(place[2] > 0, total, 0.0)
-        return turn_s[1].T
+                turn_s[phase, odd_rows, :] = jnp.where(place[2] > 0, total, 0.0)
+        return turn_s[phase].T
 
     def z_add(columns, x):
         out = []
@@ -334,16 +344,7 @@
         step = dot(mat_no[layer], silu_of_half(half).astype(BF16))
         return (h_s[x].astype(F32) + step).astype(BF16).astype(F32)
 
-    middle = list(range(1, last))
-
-    def middle_edges(layer, slot):
-        for x in middle:
-            (wz,) = edges_xz(layer, [(x, 2)])
-            (wy,) = edges_y(layer, [x])
-            put(slot, x, both_z(wz) + both_y(wy), False)
-
-    turn_s[1] = jnp.zeros_like(turn_s[1])
-    middle_edges(0, 0)
+    turn_s[...] = jnp.zeros_like(turn_s)
     greetings = -1 + functools.reduce(
         lambda a, b: a * b,
         [
@@ -351,68 +352,124 @@
             for pos, size in zip(place, sizes)
         ],
     )
-
-    def layer_step(layer, carry):
-        slot = layer
-        w0, wz = edges_xz(layer, [(0, 0), (0, 2)])
-        (wy,) = edges_y(layer, [0])
-        put(slot, 0, w0 + both_z(wz) + both_y(wy), False)
-
-        @pl.when(layer == 0)
-        def _():
-            pl.semaphore_wait(barrier, greetings)
-
-        for way in x_ways:
-            if way[0] < 0:
-                start(way, slot)
-        ring = [(x, 0) for x in range(1, cx)]
-        *wx, wz = edges_xz(layer, ring + [(last, 2)])
-        (wy,) = edges_y(layer, [last])
-        wx = [w0] + wx
-        put(slot, last, wx[last - 1] + wx[last] + both_z(wz) + both_y(wy), False)
-        for way in x_ways:
-            if way[0] > 0:
-                start(way, slot)
-        for x in middle:
-            put(slot, x, wx[x - 1] + wx[x], True)
-        for side in range(2):
-            for x in range(cx):
-                ysend[slot, side, x] = p_s[slot, x, y_rows(side), :]
-        for way in y_ways:
-            start(way, slot)
-        z_faces(slot)
-        for way in z_ways:
-            start(way, slot)
-
-        @pl.when(layer + 1 < layers)
-        def _():
-            build(layer + 1)
-
-        for way in y_ways + z_ways:
-            arrive(way, slot)
-        columns = z_columns(slot)
-        for x in middle:
-            keep_nodes(x, node(layer, slot, x, columns))
-
-        @pl.when(layer + 1 < layers)
-        def _():
-            middle_edges(layer + 1, layer + 1)
-
-        for way in x_ways:
-            arrive(way, slot)
-        keep_nodes(0, node(layer, slot, 0, columns))
-        keep_nodes(last, node(layer, slot, last, columns))
-        return carry
-
-    def sent_step(layer, carry):
-        for way in ways:
-            sent(way, layer)
-        return carry
-
-    lax.fori_loop(0, layers, layer_step, 0)
-    lax.fori_loop(0, layers, sent_step, 0)
+    middle = list(range(1, last))
+
+    def run(slow):
+        fast = last - slow
+
+        def phase_of(message, sending):
+            (dx, dy, dz), tag = message
+            if dx != 0:
+                face = 0 if (dx < 0) == sending else last
+                return FAST if face == fast else SLOW
+            if dz != 0:
+                return tag
+            return FAST if tag == fast else SLOW
+
+        def order(message):
+            (dx, dy, dz), tag = message
+            return (dy != 0 or dz != 0, dz != 0)
+
+        ordered = sorted(messages, key=order)
+
+        def starts(slot, phase, first):
+            for message in ordered:
+                if phase_of(message, True) == phase and (order(message) == (False, False)) == first:
+                    start(message, slot, slow)
+
+        def arrivals(slot, phase, pick):
+            for message in ordered:
+                if phase_of(message, False) == phase and pick(message):
+                    arrive(message, slot, slow)
+
+        def face_group(face):
+            edge = 0 if face == 0 else last - 1
+            absent = [(last, 0)] if face == last else []
+            return [(edge, 0)] + absent + [(face, 2)]
+
+        def put_face(slot, face, weighted, wy):
+            shared, *absent, wz = weighted
+            total = shared + both_z(wz) + both_y(wy)
+            for extra in absent:
+                total = total + extra
+            put(slot, face, total, False)
+            put(slot, 1 if face == 0 else last - 1, shared, True)
+
+        def stage_y(slot, xs):
+            for side in range(2):
+                for x in xs:
+                    ysend[slot, side, x] = p_s[slot, x, y_rows(side), :]
+
+        def ahead_edges(layer):
+            inner = [(x, 0) for x in middle[:-1]]
+            group = [(x, 2) for x in middle] + inner
+            weighted = edges_xz(layer, group + face_group(fast))
+            wy = edges_y(layer, middle + [fast])
+            for index, x in enumerate(middle):
+                put(layer, x, both_z(weighted[index]) + both_y(wy[index]), False)
+            for index, (x, d) in enumerate(inner):
+                put(layer, x, weighted[len(middle) + index], True)
+                put(layer, x + 1, weighted[len(middle) + index], True)
+            put_face(layer, fast, weighted[len(group) :], wy[-1])
+
+        def fast_sends(slot):
+            starts(slot, FAST, True)
+            stage_y(slot, [fast])
+            z_faces(slot, [fast], FAST)
+            starts(slot, FAST, False)
+
+        ahead_edges(0)
+        pl.semaphore_wait(barrier, greetings)
+        fast_sends(0)
+
+        def layer_step(layer, carry):
+            slot = layer
+            weighted = edges_xz(layer, face_group(slow))
+            (wy,) = edges_y(layer, [slow])
+            put_face(slot, slow, weighted, wy)
+            starts(slot, SLOW, True)
+            stage_y(slot, [slow] + middle)
+            z_faces(slot, [slow] + middle, SLOW)
+            starts(slot, SLOW, False)
+
+            @pl.when(layer + 1 < layers)
+            def _():
+                build(layer + 1)
+
+            arrivals(slot, FAST, lambda message: True)
+            columns = z_columns(slot, fast, FAST)
+            keep_nodes(fast, node(layer, slot, fast, columns))
+
+            def late(message):
+                (dx, dy, dz), tag = message
+                return dz == 0 and (dx != 0 or tag == slow)
+
+            arrivals(slot, SLOW, lambda message: not late(message))
+            columns = z_columns(slot, slow, SLOW)
+            for x in middle:
+                keep_nodes(x, node(layer, slot, x, columns))
+
+            @pl.when(layer + 1 < layers)
+            def _():
+                ahead_edges(layer + 1)
+                fast_sends(layer + 1)
+
+            arrivals(slot, SLOW, late)
+            keep_nodes(slow, node(layer, slot, slow, columns))
+            return carry
+
+        def sent_step(layer, carry):
+            for message in messages:
+                sent(message, layer, slow)
+            return carry
+
+        lax.fori_loop(0, layers, layer_step, 0)
+        lax.fori_loop(0, layers, sent_step, 0)
+
+    pl.when(lax.rem(place[0], 2) == 0)(lambda: run(0))
+    pl.when(lax.rem(place[0], 2) == 1)(lambda: run(last))
     for x in range(cx):
-        out_ref[:, x] = h_s[x].astype(F32).reshape(chans, cy, cz).astype(BF16)
+        out_ref[:, x] = h_s[x].astype(F32).reshape(chans, cy, cz)
 
 
 def solution(mesh):
@@ -422,9 +479,9 @@
         layers = params[0].shape[0]
         chans, cx, cy, cz = features.shape
         rows = chans * cy
-        assert cz == 128 and rows % 128 == 0 and cy % 8 == 0 and cx > 1
+        assert cz == 128 and rows % 128 == 0 and cy % 8 == 0 and cx > 2
         slots = layers
-        ways = len(ways_of(sizes))
+        ways = len(messages_of(sizes, cx))
         zrows = -(-cx * (rows // 128) // 8) * 8
         vmem = pl.BlockSpec(memory_space=pltpu.VMEM)
         scratch = [pltpu.VMEM(a.shape, a.dtype) for a in (features, edge_state, multiplicity, *params)]
@@ -442,19 +499,19 @@
             pltpu.VMEM((layers, rows, cz), F32),
             pltpu.VMEM((layers, rows, cz), F32),
             pltpu.VMEM((slots, 2, cx, chans, cz), F32),
-            pltpu.VMEM((slots, 2, zrows, 128), F32),
+            pltpu.VMEM((slots, 2, 2, zrows, 128), F32),
             pltpu.VMEM((slots, 2, rows, cz), F32),
             pltpu.VMEM((slots, 2, cx, chans, cz), F32),
             pltpu.VMEM((slots, 4, chans, cz), F32),
-            pltpu.VMEM((slots, 2, 9, zrows, 128), F32),
-            pltpu.VMEM((2, 128, 128), F32),
+            pltpu.VMEM((slots, 2, 4, 3, zrows, 128), F32),
+            pltpu.VMEM((3, 128, 128), F32),
             pltpu.SemaphoreType.DMA((9,)),
             pltpu.SemaphoreType.DMA((slots, ways)),
             pltpu.SemaphoreType.DMA((slots, ways)),
         ]
-        return pl.pallas_call(
+        nodes = pl.pallas_call(
             functools.partial(kernel, sizes, layers),
-            out_shape=jax.ShapeDtypeStruct(features.shape, features.dtype),
+            out_shape=jax.ShapeDtypeStruct(features.shape, F32),
             in_specs=[pl.BlockSpec(memory_space=pltpu.HBM)] * 9,
             out_specs=vmem,
             scratch_shapes=scratch,
@@ -462,6 +519,7 @@
                 collective_id=0, has_side_effects=True, vmem_limit_bytes=60 * 1024 * 1024
             ),
         )(features, edge_state, multiplicity, *params)
+        return nodes.astype(features.dtype)
 
     placed = (P(None, *AXES), P(None, None, *AXES), P(*AXES)) + (P(),) * 6
     return jax.shard_map(

time: 34 us -> 31 us (0.912)
  Pallas kernels: 32.1 us -> 29.1 us
  other arithmetic: 0 us -> 1.7 us
  local copies, waits for them, and re-layouts: 1.62 us -> 0 us
    pallas_call x1, Pallas kernels: 32.1 us -> 29.1 us  [on_device(): pl.pallas_call(functools.partial(kernel, sizes, layers), out_shape=jax.Sh...]
    convert_element_type x0 -> x1, other arithmetic: none -> 1.7 us  [on_device(): return nodes.astype(features.dtype)]
    unnamed x1 -> x0, local copies, waits for them, and re-layouts: 1.62 us -> none
where the time goes in v3:
time: 31 us; the launch traced here: 30.8 us
  Pallas kernels  29.1 us (94%)
  other arithmetic  1.7 us (5%)
    pallas_call x1, Pallas kernels, on_device(): pl.pallas_call(functools.partial(kernel, sizes, layers), out_shape=jax.Sh...  29.1 us
    convert_element_type x1, other arithmetic, on_device(): return nodes.astype(features.dtype)  1.7 us

profile of v3, /device:TPU:1, one launch (start us, length us, event | category | flops | bytes accessed | tf_op | source)
XLA Modules:
  0.0 30.8 jit_solution(18394418359833020308)
XLA Ops:
  0.0 29.1 %shard_map.91 = f32[32,3,8,128]{3,2,1,0:T(8,128)} custom-call(bf16[32,3,8,128]{3,2,1,0:T(8,128)(2,1)} %feat_hbm.1, bf16[3,32,3,8,128]{4,3,2,1,0:T(8,128)(2,1)} %edge_hbm.1, s32[3,8,128]{2,1,0:T(8,128)} %mult_hbm.1, bf16[3,32,96]{2,1,0:T(8,128)(2,1)} %win_hbm.1, bf16[3,32,32]{2,1,0:T(8,128)(2,1)} %wout_hbm.1, f32[3,32]{1,0:T(4,128)} %bin_hbm.1, ...), custom_call_target="tpu_custom_call" | custom-call | tf_op jit(solution)/shard_map/pallas_call | solution.py:512
  29.1 1.7 %convert_element_type.3 = bf16[32,3,8,128]{3,2,1,0:T(8,128)(2,1)} convert(f32[32,3,8,128]{3,2,1,0:T(8,128)} %shard_map.91) | non-fusion elementwise | flops 98304 | bytes 589824 | tf_op jit(solution)/shard_map/convert_element_type | solution.py:522

commit v4 on v3

--- a/solution.py
+++ b/solution.py
@@ -36,14 +36,11 @@
     ]
 
 
-def messages_of(sizes, cx):
+def messages_of(sizes):
     out = []
     for way in ways_of(sizes):
         dx, dy, dz = way
-        tags = (None,)
-        if dx == 0:
-            tags = (FAST, SLOW) if dz != 0 else range(cx)
-        out += [(way, tag) for tag in tags]
+        out += [(way, tag) for tag in ((FAST, SLOW) if dx == 0 else (None,))]
     return out
 
 
@@ -100,7 +97,7 @@
             pl.when(there)(act)
 
     ways = ways_of(sizes)
-    messages = messages_of(sizes, cx)
+    messages = messages_of(sizes)
     z_steps = [way[2] for way in ways if way[0] == 0 and way[1] == 0 and way[2] != 0]
 
     xrx[...] = jnp.zeros_like(xrx)
@@ -242,8 +239,9 @@
             source = p_s.at[slot, face]
             target = xrx.at[slot, 0 if dx < 0 else 1]
         elif dx == 0:
-            source = ysend.at[slot, side, tag]
-            target = yrx.at[slot, side, tag]
+            slabs = pl.ds(last - slow, 1) if tag == FAST else pl.ds(0 if slow == 0 else 1, last)
+            source = ysend.at[slot, side, slabs]
+            target = yrx.at[slot, side, slabs]
         else:
             source = ysend.at[slot, side, face]
             target = xyrx.at[slot, (0 if dx < 0 else 2) + side]
@@ -362,9 +360,7 @@
             if dx != 0:
                 face = 0 if (dx < 0) == sending else last
                 return FAST if face == fast else SLOW
-            if dz != 0:
-                return tag
-            return FAST if tag == fast else SLOW
+            return tag
 
         def order(message):
             (dx, dy, dz), tag = message
@@ -382,17 +378,17 @@
                 if phase_of(message, False) == phase and pick(message):
                     arrive(message, slot, slow)
 
-        def face_group(face):
-            edge = 0 if face == 0 else last - 1
-            absent = [(last, 0)] if face == last else []
-            return [(edge, 0)] + absent + [(face, 2)]
-
-        def put_face(slot, face, weighted, wy):
-            shared, *absent, wz = weighted
-            total = shared + both_z(wz) + both_y(wy)
-            for extra in absent:
-                total = total + extra
-            put(slot, face, total, False)
+        def shared_edge(face):
+            return (0 if face == 0 else last - 1, 0)
+
+        def own_edges(face):
+            return ([(last, 0)] if face == last else []) + [(face, 2)]
+
+        def inside(weighted, wy):
+            *absent, wz = weighted
+            return sum(absent, both_z(wz) + both_y(wy))
+
+        def put_shared(slot, face, shared):
             put(slot, 1 if face == 0 else last - 1, shared, True)
 
         def stage_y(slot, xs):
@@ -400,17 +396,24 @@
                 for x in xs:
                     ysend[slot, side, x] = p_s[slot, x, y_rows(side), :]
 
-        def ahead_edges(layer):
+        def fast_edges(layer):
+            weighted = edges_xz(layer, own_edges(fast))
+            (wy,) = edges_y(layer, [fast])
+            put(layer, fast, inside(weighted, wy), False)
+
+        def middle_edges(layer):
             inner = [(x, 0) for x in middle[:-1]]
-            group = [(x, 2) for x in middle] + inner
-            weighted = edges_xz(layer, group + face_group(fast))
-            wy = edges_y(layer, middle + [fast])
+            group = [(x, 2) for x in middle] + [shared_edge(fast)] + inner
+            weighted = edges_xz(layer, group)
+            wy = edges_y(layer, middle)
             for index, x in enumerate(middle):
                 put(layer, x, both_z(weighted[index]) + both_y(wy[index]), False)
-            for index, (x, d) in enumerate(inner):
-                put(layer, x, weighted[len(middle) + index], True)
-                put(layer, x + 1, weighted[len(middle) + index], True)
-            put_face(layer, fast, weighted[len(group) :], wy[-1])
+            shared, *inner_weighted = weighted[len(middle) :]
+            for (x, d), value in zip(inner, inner_weighted):
+                put(layer, x, value, True)
+                put(layer, x + 1, value, True)
+            put(layer, fast, shared, True)
+            put_shared(layer, fast, shared)
 
         def fast_sends(slot):
             starts(slot, FAST, True)
@@ -418,16 +421,18 @@
             z_faces(slot, [fast], FAST)
             starts(slot, FAST, False)
 
-        ahead_edges(0)
+        fast_edges(0)
+        middle_edges(0)
         pl.semaphore_wait(barrier, greetings)
         fast_sends(0)
 
         def layer_step(layer, carry):
             slot = layer
-            weighted = edges_xz(layer, face_group(slow))
+            shared, *weighted = edges_xz(layer, [shared_edge(slow)] + own_edges(slow))
             (wy,) = edges_y(layer, [slow])
-            put_face(slot, slow, weighted, wy)
+            put(slot, slow, shared + inside(weighted, wy), False)
             starts(slot, SLOW, True)
+            put_shared(slot, slow, shared)
             stage_y(slot, [slow] + middle)
             z_faces(slot, [slow] + middle, SLOW)
             starts(slot, SLOW, False)
@@ -440,9 +445,13 @@
             columns = z_columns(slot, fast, FAST)
             keep_nodes(fast, node(layer, slot, fast, columns))
 
+            @pl.when(layer + 1 < layers)
+            def _():
+                fast_edges(layer + 1)
+
             def late(message):
                 (dx, dy, dz), tag = message
-                return dz == 0 and (dx != 0 or tag == slow)
+                return dz == 0 and dx != 0
 
             arrivals(slot, SLOW, lambda message: not late(message))
             columns = z_columns(slot, slow, SLOW)
@@ -451,25 +460,21 @@
 
             @pl.when(layer + 1 < layers)
             def _():
-                ahead_edges(layer + 1)
+                middle_edges(layer + 1)
                 fast_sends(layer + 1)
 
+            for message in messages:
+                sent(message, layer, slow)
             arrivals(slot, SLOW, late)
             keep_nodes(slow, node(layer, slot, slow, columns))
             return carry
 
-        def sent_step(layer, carry):
-            for message in messages:
-                sent(message, layer, slow)
-            return carry
-
         lax.fori_loop(0, layers, layer_step, 0)
-        lax.fori_loop(0, layers, sent_step, 0)
 
     pl.when(lax.rem(place[0], 2) == 0)(lambda: run(0))
     pl.when(lax.rem(place[0], 2) == 1)(lambda: run(last))
     for x in range(cx):
-        out_ref[:, x] = h_s[x].astype(F32).reshape(chans, cy, cz)
+        out_ref[:, x] = h_s[x].astype(F32).reshape(chans, cy, cz).astype(BF16)
 
 
 def solution(mesh):
@@ -481,7 +486,7 @@
         rows = chans * cy
         assert cz == 128 and rows % 128 == 0 and cy % 8 == 0 and cx > 2
         slots = layers
-        ways = len(messages_of(sizes, cx))
+        ways = len(messages_of(sizes))
         zrows = -(-cx * (rows // 128) // 8) * 8
         vmem = pl.BlockSpec(memory_space=pltpu.VMEM)
         scratch = [pltpu.VMEM(a.shape, a.dtype) for a in (features, edge_state, multiplicity, *params)]
@@ -509,9 +514,9 @@
             pltpu.SemaphoreType.DMA((slots, ways)),
             pltpu.SemaphoreType.DMA((slots, ways)),
         ]
-        nodes = pl.pallas_call(
+        return pl.pallas_call(
             functools.partial(kernel, sizes, layers),
-            out_shape=jax.ShapeDtypeStruct(features.shape, F32),
+            out_shape=pltpu.VMEM(features.shape, features.dtype),
             in_specs=[pl.BlockSpec(memory_space=pltpu.HBM)] * 9,
             out_specs=vmem,
             scratch_shapes=scratch,
@@ -519,7 +524,6 @@
                 collective_id=0, has_side_effects=True, vmem_limit_bytes=60 * 1024 * 1024
             ),
         )(features, edge_state, multiplicity, *params)
-        return nodes.astype(features.dtype)
 
     placed = (P(None, *AXES), P(None, None, *AXES), P(*AXES)) + (P(),) * 6
     return jax.shard_map(

time: 31 us -> 30 us (0.968)
  other arithmetic: 1.7 us -> 0 us
  local copies, waits for them, and re-layouts: 0 us -> 0.68 us
    convert_element_type x1 -> x0, other arithmetic: 1.7 us -> none  [on_device(): return nodes.astype(features.dtype)]
    unnamed x0 -> x1, local copies, waits for them, and re-layouts: none -> 0.68 us
where the time goes in v4:
time: 30 us; the launch traced here: 29.9 us
  Pallas kernels  29.2 us (97%)
  local copies, waits for them, and re-layouts  0.68 us (2%)
    pallas_call x1, Pallas kernels, on_device(): pl.pallas_call(functools.partial(kernel, sizes, layers), out_shape=pltpu....  29.2 us
    unnamed x1, local copies, waits for them, and re-layouts  0.68 us

profile of v4, /device:TPU:1, one launch (start us, length us, event | category | flops | bytes accessed | tf_op | source)
XLA Modules:
  0.0 29.9 jit_solution(16444626684597715633)
XLA Ops:
  0.0 29.2 %shard_map.91 = bf16[32,3,8,128]{3,2,1,0:T(8,128)(2,1)S(1)} custom-call(bf16[32,3,8,128]{3,2,1,0:T(8,128)(2,1)} %feat_hbm.1, bf16[3,32,3,8,128]{4,3,2,1,0:T(8,128)(2,1)} %edge_hbm.1, s32[3,8,128]{2,1,0:T(8,128)} %mult_hbm.1, bf16[3,32,96]{2,1,0:T(8,128)(2,1)} %win_hbm.1, bf16[3,32,32]{2,1,0:T(8,128)(2,1)} %wout_hbm.1, f32[3,32]{1,0:T(4,128)} %bin_hbm.1, ...), custom_call_target="tpu_custom_call" | custom-call | tf_op jit(solution)/shard_map/pallas_call | solution.py:517
  29.2 0.7 %copy.11 = bf16[32,3,8,128]{3,2,1,0:T(8,128)(2,1)} copy(bf16[32,3,8,128]{3,2,1,0:T(8,128)(2,1)S(1)} %shard_map.91) | data formatting | bytes 393216

commit v5 on v4

--- a/solution.py
+++ b/solution.py
@@ -50,8 +50,8 @@
     feat_hbm, edge_hbm, mult_hbm, win_hbm, wout_hbm, bin_hbm, nin_hbm, nout_hbm, bnode_hbm,
     out_ref,
     feat_ref, edge_ref, mult_ref, win_ref, wout_ref, bin_ref, nin_ref, nout_ref, bnode_ref,
-    h_s, hz_s, e_s, w_s, p_s, inc_s, mat_e, mat_o, mat_n, mat_no, bias_e, bias_n,
-    ysend, zsend, xrx, yrx, xyrx, zrx, turn_s, in_sem, send_sem, recv_sem,
+    stage_s, h_s, hz_s, e_s, w_s, p_s, bias_e, bias_n,
+    zsend, xrx, yrx, xyrx, zrx, turn_s, in_sem, send_sem, recv_sem,
 ):
     loads = [
         pltpu.make_async_copy(source, target, in_sem.at[index])
@@ -65,8 +65,9 @@
         load.start()
 
     chans, cx, cy, cz = feat_ref.shape
-    rows = chans * cy
+    rows, cells = chans * cy, cy * cz
     halves = rows // 128
+    per_half = cy // halves
     last = cx - 1
     zrows = zsend.shape[3]
     place = [lax.axis_index(axis) for axis in AXES]
@@ -112,52 +113,23 @@
 
         when_exists(way, greet)
 
-    mine = iota((rows, chans), 0) // cy == iota((rows, chans), 1)
-    spread = mine.astype(F32).astype(BF16)
-    row_y, col_y = iota((cy, rows), 0), iota((cy, rows), 1) % cy
-    same_y = (row_y == col_y).astype(F32)
-    half_same, half_next = 0.5 * same_y, 0.5 * (row_y + 1 == col_y).astype(F32)
-    col_c = iota((1, rows), 1) // cy
-
-    def widen(weights):
-        width = weights.shape[1]
-        parts = []
-        for part in range(width // chans):
-            pick = iota((width, rows), 0) == part * chans + col_c
-            parts.append(dot(weights, pick.astype(F32).astype(BF16)).astype(BF16))
-        return parts
-
-    def build(layer):
-        wide = widen(win_ref[layer]) + widen(wout_ref[layer])
-        wide += widen(nin_ref[layer]) + widen(nout_ref[layer])
-
-        def block(index):
-            return dot(spread, wide[index]).reshape(chans, cy, rows)
-
-        def flat(values):
-            return values.reshape(rows, rows).astype(BF16)
-
-        own, other = block(0), block(1)
-        own_same = own * half_same[None]
-        mat_e[layer, :, 0:rows] = flat(own_same)
-        mat_e[layer, :, rows : 2 * rows] = flat(other * half_same[None])
-        mat_e[layer, :, 2 * rows : 3 * rows] = flat(block(2) * half_same[None])
-        mat_e[layer, :, 3 * rows :] = flat(own_same + other * half_next[None])
-        mat_o[layer] = flat(block(3) * same_y[None])
-        mat_n[layer, :, 0:rows] = flat(block(4) * half_same[None])
-        mat_n[layer, :, rows:] = flat(block(5) * half_same[None])
-        mat_no[layer] = flat(block(6) * same_y[None])
-        for source, target in ((bin_ref, bias_e), (bnode_ref, bias_n)):
-            column = jnp.sum(
-                jnp.where(mine, source[pl.ds(layer, 1), :], 0.0), axis=1, keepdims=True
-            )
-            target[layer] = jnp.broadcast_to(0.5 * column, (rows, cz))
-
-    for load in loads[:6]:
+    def at_y(values, y):
+        return values[:, y * cz : (y + 1) * cz]
+
+    def over_y(make):
+        return jnp.concatenate([make(y) for y in range(cy)], axis=1)
+
+    for load in loads[:7]:
         load.wait()
-    build(0)
-    for load in loads[6:]:
-        load.wait()
+    diagonal = iota((chans, chans), 0) == iota((chans, chans), 1)
+    for source, target in ((bin_ref, bias_e), (bnode_ref, bias_n)):
+        for layer in range(layers):
+            row = source[layer : layer + 1, :]
+            column = jnp.sum(jnp.where(diagonal, row, 0.0), axis=1, keepdims=True)
+            target[layer] = jnp.broadcast_to(0.5 * column, (chans, cz))
+
+    def halved(weights):
+        return (0.5 * weights.astype(F32)).astype(BF16)
 
     fluid = mult_ref[1, 1:2, 1:2] > 0
     zeros = jnp.zeros((cy, cz), jnp.int32)
@@ -170,60 +142,66 @@
         )
         for d in range(3):
             shared = jnp.minimum(count, ahead[d])
-            w_s[d, x] = jnp.where(
+            weight = jnp.where(
                 fluid & (shared > 0), 1.0 / jnp.maximum(shared, 1).astype(F32), 0.0
             )
-
-    before_end = iota((rows, cz), 1) < cz - 1
+            w_s[d, x] = over_y(lambda y: jnp.broadcast_to(weight[y : y + 1], (8, cz)))
+
+    before_end = iota((chans, cz), 1) < cz - 1
 
     def keep_nodes(x, values):
         h_s[x] = values.astype(BF16)
-        hz_s[x] = jnp.where(before_end, pltpu.roll(values, cz - 1, 1), 0.0).astype(BF16)
-
+        hz_s[x] = over_y(
+            lambda y: jnp.where(before_end, pltpu.roll(at_y(values, y), cz - 1, 1), 0.0)
+        ).astype(BF16)
+
+    def channel_rows(index, values):
+        stage_s[index] = values.astype(F32).reshape(rows, cz)
+        return over_y(lambda y: stage_s[index, pl.ds(y, chans, stride=cy), :])
+
+    loads[7].wait()
     for x in range(cx):
-        keep_nodes(x, feat_ref[:, x].astype(F32).reshape(rows, cz))
+        keep_nodes(x, channel_rows(x, feat_ref[:, x]))
+    loads[8].wait()
+    for x in range(cx):
         for d in range(3):
-            e_s[d, x] = edge_ref[d, :, x].astype(F32).reshape(rows, cz).astype(BF16)
-
-    def finish(layer, slabs, half):
-        count = len(slabs)
-        half = half + jnp.concatenate([bias_e[layer]] * count, axis=1)
-        message = dot(mat_o[layer], silu_of_half(half).astype(BF16))
+            index = (1 + d) * cx + x
+            e_s[d, x] = channel_rows(index, edge_ref[d, :, x]).astype(BF16)
+
+    def next_nodes(x, d):
+        if d == 2:
+            return hz_s[x]
+        if d == 1:
+            return jnp.concatenate([h_s[x][:, cz:], jnp.zeros((chans, cz), BF16)], axis=1)
+        return h_s[x + 1] if x < last else jnp.zeros((chans, cells), BF16)
+
+    def edges(layer, slabs):
+        weight_in, weight_out = halved(win_ref[layer]), wout_ref[layer]
+        bias = jnp.concatenate([bias_e[layer]] * cy, axis=1)
         weighted = []
-        for index, (x, d) in enumerate(slabs):
-            own = message[:, index * cz : (index + 1) * cz]
-            e_s[d, x] = (e_s[d, x].astype(F32) + own).astype(BF16)
-            weighted.append(w_s[d, x][None] * own.reshape(chans, cy, cz))
+        for x, d in slabs:
+            edge = e_s[d, x]
+            stacked = jnp.concatenate([h_s[x], next_nodes(x, d), edge], axis=0)
+            half = dot(weight_in, stacked) + bias
+            message = dot(weight_out, silu_of_half(half).astype(BF16))
+            e_s[d, x] = (edge.astype(F32) + message).astype(BF16)
+            spread = message.reshape(chans // 8, 8, cells) * w_s[d, x][None]
+            weighted.append(spread.reshape(chans, cells))
         return weighted
 
-    def edges_xz(layer, slabs):
-        nothing = jnp.zeros((rows, cz), BF16)
-        own = jnp.concatenate([h_s[x] for x, d in slabs], axis=1)
-        other = jnp.concatenate(
-            [hz_s[x] if d == 2 else h_s[x + 1] if x < last else nothing for x, d in slabs], axis=1
+    def both_y(weighted):
+        return weighted + jnp.concatenate(
+            [jnp.zeros((chans, cz), F32), weighted[:, : cells - cz]], axis=1
         )
-        edge = jnp.concatenate([e_s[d, x] for x, d in slabs], axis=1)
-        stacked = jnp.concatenate([own, other, edge], axis=0)
-        return finish(layer, slabs, dot(mat_e[layer, :, 0 : 3 * rows], stacked))
-
-    def edges_y(layer, xs):
-        edge = jnp.concatenate([e_s[1, x] for x in xs], axis=1)
-        own = jnp.concatenate([h_s[x] for x in xs], axis=1)
-        stacked = jnp.concatenate([edge, own], axis=0)
-        slabs = [(x, 1) for x in xs]
-        return finish(layer, slabs, dot(mat_e[layer, :, 2 * rows :], stacked))
-
-    def both_y(weighted):
-        return weighted + pltpu.roll(weighted, 1, 1)
 
     def both_z(weighted):
-        return weighted + pltpu.roll(weighted, 1, 2)
+        return weighted + over_y(lambda y: pltpu.roll(at_y(weighted, y), 1, 1))
 
     def put(slot, x, value, add):
-        value = value.reshape(rows, cz)
-        if add:
-            value = p_s[slot, x] + value
-        p_s[slot, x] = value
+        p_s[slot, x] = p_s[slot, x] + value if add else value
+
+    def edge_lanes(side):
+        return pl.ds(0 if side == 0 else cells - cz, cz)
 
     def transfer(message, slot, slow):
         way, tag = message
@@ -240,10 +218,10 @@
             target = xrx.at[slot, 0 if dx < 0 else 1]
         elif dx == 0:
             slabs = pl.ds(last - slow, 1) if tag == FAST else pl.ds(0 if slow == 0 else 1, last)
-            source = ysend.at[slot, side, slabs]
+            source = p_s.at[slot, slabs, :, edge_lanes(side)]
             target = yrx.at[slot, side, slabs]
         else:
-            source = ysend.at[slot, side, face]
+            source = p_s.at[slot, face, :, edge_lanes(side)]
             target = xyrx.at[slot, (0 if dx < 0 else 2) + side]
         return pltpu.make_async_remote_copy(
             src_ref=source,
@@ -271,7 +249,11 @@
         for x in xs:
             for part in range(halves):
                 at = 2 * (x * halves + part)
-                piece = pltpu.roll(p_s[slot, x, part * 128 : (part + 1) * 128], at + 1, 1)
+                whole = p_s[slot, x]
+                piece = jnp.concatenate(
+                    [at_y(whole, part * per_half + y) for y in range(per_half)], axis=0
+                )
+                piece = pltpu.roll(piece, at + 1, 1)
                 faces = jnp.where((lane == at) | (lane == at + 1), piece, faces)
         turn_s[2] = faces.T
         first, final = turn_s[2, odd_rows, :], turn_s[2, even_rows, :]
@@ -285,7 +267,7 @@
 
     def z_total(slot, which, face, phase):
         total = jnp.zeros((zrows, 128), F32)
-        shift_x, shift_y = last * halves, cy - 1
+        shift_x = last * halves
         for dy in STEPS:
             part = zrx[slot, which, 1 + phase, dy + 1]
             if face == 0:
@@ -297,9 +279,12 @@
                 piece = jnp.where(inside, pltpu.roll(piece, shift_x, 0), 0.0)
             part = part + piece
             if dy > 0:
-                part = jnp.where(lane_z % cy == 0, pltpu.roll(part, 128 - shift_y, 1), 0.0)
+                part = pltpu.roll(pltpu.roll(part, chans % 128, 1), zrows - halves + 1, 0)
+                part = jnp.where((row_z % halves == 0) & (lane_z < chans), part, 0.0)
             if dy < 0:
-                part = jnp.where(lane_z % cy == cy - 1, pltpu.roll(part, shift_y, 1), 0.0)
+                part = pltpu.roll(pltpu.roll(part, 128 - chans, 1), halves - 1, 0)
+                inside = (row_z % halves == halves - 1) & (lane_z >= 128 - chans)
+                part = jnp.where(inside, part, 0.0)
             total = total + part
         return total
 
@@ -318,10 +303,9 @@
             at = 2 * (x * halves + part)
             piece = pltpu.roll(columns, cz - at - 1, 1)
             out.append(jnp.where((lane == 0) | (lane == cz - 1), piece, 0.0))
-        return jnp.concatenate(out, axis=0)
-
-    def y_rows(side):
-        return pl.ds(0 if side == 0 else cy - 1, chans, stride=cy)
+        return over_y(
+            lambda y: out[y // per_half][y % per_half * chans : (y % per_half + 1) * chans]
+        )
 
     def node(layer, slot, x, columns):
         total = p_s[slot, x] + z_add(columns, x)
@@ -329,17 +313,19 @@
             total = total + xrx[slot, 1]
         if x == last:
             total = total + xrx[slot, 0]
-        inc_s[x] = total
+        blocks = [at_y(total, y) for y in range(cy)]
         for side in range(2):
             extra = yrx[slot, 1 - side, x]
             if x == 0:
                 extra = extra + xyrx[slot, 2 + (1 - side)]
             if x == last:
                 extra = extra + xyrx[slot, 1 - side]
-            inc_s[x, y_rows(side), :] = inc_s[x, y_rows(side), :] + extra
-        stacked = jnp.concatenate([h_s[x], inc_s[x].astype(BF16)], axis=0)
-        half = dot(mat_n[layer], stacked) + bias_n[layer]
-        step = dot(mat_no[layer], silu_of_half(half).astype(BF16))
+            blocks[-side] = blocks[-side] + extra
+        incoming = jnp.concatenate(blocks, axis=1).astype(BF16)
+        stacked = jnp.concatenate([h_s[x], incoming], axis=0)
+        half = dot(halved(nin_ref[layer]), stacked)
+        half = half + jnp.concatenate([bias_n[layer]] * cy, axis=1)
+        step = dot(nout_ref[layer], silu_of_half(half).astype(BF16))
         return (h_s[x].astype(F32) + step).astype(BF16).astype(F32)
 
     turn_s[...] = jnp.zeros_like(turn_s)
@@ -382,34 +368,24 @@
             return (0 if face == 0 else last - 1, 0)
 
         def own_edges(face):
-            return ([(last, 0)] if face == last else []) + [(face, 2)]
-
-        def inside(weighted, wy):
-            *absent, wz = weighted
+            return ([(last, 0)] if face == last else []) + [(face, 2), (face, 1)]
+
+        def inside(weighted):
+            *absent, wz, wy = weighted
             return sum(absent, both_z(wz) + both_y(wy))
 
         def put_shared(slot, face, shared):
             put(slot, 1 if face == 0 else last - 1, shared, True)
 
-        def stage_y(slot, xs):
-            for side in range(2):
-                for x in xs:
-                    ysend[slot, side, x] = p_s[slot, x, y_rows(side), :]
-
         def fast_edges(layer):
-            weighted = edges_xz(layer, own_edges(fast))
-            (wy,) = edges_y(layer, [fast])
-            put(layer, fast, inside(weighted, wy), False)
+            put(layer, fast, inside(edges(layer, own_edges(fast))), False)
 
         def middle_edges(layer):
             inner = [(x, 0) for x in middle[:-1]]
-            group = [(x, 2) for x in middle] + [shared_edge(fast)] + inner
-            weighted = edges_xz(layer, group)
-            wy = edges_y(layer, middle)
-            for index, x in enumerate(middle):
-                put(layer, x, both_z(weighted[index]) + both_y(wy[index]), False)
-            shared, *inner_weighted = weighted[len(middle) :]
-            for (x, d), value in zip(inner, inner_weighted):
+            for x in middle:
+                put(layer, x, inside(edges(layer, [(x, 2), (x, 1)])), False)
+            shared, *weighted = edges(layer, [shared_edge(fast)] + inner)
+            for (x, d), value in zip(inner, weighted):
                 put(layer, x, value, True)
                 put(layer, x + 1, value, True)
             put(layer, fast, shared, True)
@@ -417,7 +393,6 @@
 
         def fast_sends(slot):
             starts(slot, FAST, True)
-            stage_y(slot, [fast])
             z_faces(slot, [fast], FAST)
             starts(slot, FAST, False)
 
@@ -428,18 +403,12 @@
 
         def layer_step(layer, carry):
             slot = layer
-            shared, *weighted = edges_xz(layer, [shared_edge(slow)] + own_edges(slow))
-            (wy,) = edges_y(layer, [slow])
-            put(slot, slow, shared + inside(weighted, wy), False)
+            shared, *weighted = edges(layer, [shared_edge(slow)] + own_edges(slow))
+            put(slot, slow, shared + inside(weighted), False)
             starts(slot, SLOW, True)
             put_shared(slot, slow, shared)
-            stage_y(slot, [slow] + middle)
             z_faces(slot, [slow] + middle, SLOW)
             starts(slot, SLOW, False)
-
-            @pl.when(layer + 1 < layers)
-            def _():
-                build(layer + 1)
 
             arrivals(slot, FAST, lambda message: True)
             columns = z_columns(slot, fast, FAST)
@@ -474,7 +443,10 @@
     pl.when(lax.rem(place[0], 2) == 0)(lambda: run(0))
     pl.when(lax.rem(place[0], 2) == 1)(lambda: run(last))
     for x in range(cx):
-        out_ref[:, x] = h_s[x].astype(F32).reshape(chans, cy, cz).astype(BF16)
+        final = h_s[x].astype(F32)
+        for y in range(cy):
+            stage_s[x, pl.ds(y, chans, stride=cy), :] = at_y(final, y)
+        out_ref[:, x] = stage_s[x].reshape(chans, cy, cz).astype(BF16)
 
 
 def solution(mesh):
@@ -483,29 +455,25 @@
     def on_device(features, edge_state, multiplicity, *params):
         layers = params[0].shape[0]
         chans, cx, cy, cz = features.shape
-        rows = chans * cy
+        rows, cells = chans * cy, cy * cz
         assert cz == 128 and rows % 128 == 0 and cy % 8 == 0 and cx > 2
+        assert chans % 16 == 0 and 128 % chans == 0 and cx * rows <= 64 * 128
         slots = layers
         ways = len(messages_of(sizes))
         zrows = -(-cx * (rows // 128) // 8) * 8
         vmem = pl.BlockSpec(memory_space=pltpu.VMEM)
         scratch = [pltpu.VMEM(a.shape, a.dtype) for a in (features, edge_state, multiplicity, *params)]
         scratch += [
-            pltpu.VMEM((cx, rows, cz), BF16),
-            pltpu.VMEM((cx, rows, cz), BF16),
-            pltpu.VMEM((3, cx, rows, cz), BF16),
-            pltpu.VMEM((3, cx, cy, cz), F32),
-            pltpu.VMEM((slots, cx, rows, cz), F32),
-            pltpu.VMEM((cx, rows, cz), F32),
-            pltpu.VMEM((layers, rows, 4 * rows), BF16),
-            pltpu.VMEM((layers, rows, rows), BF16),
-            pltpu.VMEM((layers, rows, 2 * rows), BF16),
-            pltpu.VMEM((layers, rows, rows), BF16),
-            pltpu.VMEM((layers, rows, cz), F32),
-            pltpu.VMEM((layers, rows, cz), F32),
-            pltpu.VMEM((slots, 2, cx, chans, cz), F32),
+            pltpu.VMEM((4 * cx, rows, cz), F32),
+            pltpu.VMEM((cx, chans, cells), BF16),
+            pltpu.VMEM((cx, chans, cells), BF16),
+            pltpu.VMEM((3, cx, chans, cells), BF16),
+            pltpu.VMEM((3, cx, 8, cells), F32),
+            pltpu.VMEM((slots, cx, chans, cells), F32),
+            pltpu.VMEM((layers, chans, cz), F32),
+            pltpu.VMEM((layers, chans, cz), F32),
             pltpu.VMEM((slots, 2, 2, zrows, 128), F32),
-            pltpu.VMEM((slots, 2, rows, cz), F32),
+            pltpu.VMEM((slots, 2, chans, cells), F32),
             pltpu.VMEM((slots, 2, cx, chans, cz), F32),
             pltpu.VMEM((slots, 4, chans, cz), F32),
             pltpu.VMEM((slots, 2, 4, 3, zrows, 128), F32),

time: 30 us -> 28.2 us (0.940)
  Pallas kernels: 29.2 us -> 27.4 us
    pallas_call x1, Pallas kernels: 29.2 us -> 27.4 us  [on_device(): pl.pallas_call(functools.partial(kernel, sizes, layers), out_shape=pltpu....]
where the time goes in v5:
time: 28.2 us; the launch traced here: 28.1 us
  Pallas kernels  27.4 us (97%)
  local copies, waits for them, and re-layouts  0.68 us (2%)
    pallas_call x1, Pallas kernels, on_device(): pl.pallas_call(functools.partial(kernel, sizes, layers), out_shape=pltpu....  27.4 us
    unnamed x1, local copies, waits for them, and re-layouts  0.68 us

profile of v5, /device:TPU:1, one launch (start us, length us, event | category | flops | bytes accessed | tf_op | source)
XLA Modules:
  0.0 28.1 jit_solution(11607352576547405250)
XLA Ops:
  0.0 27.4 %shard_map.91 = bf16[32,3,8,128]{3,2,1,0:T(8,128)(2,1)S(1)} custom-call(bf16[32,3,8,128]{3,2,1,0:T(8,128)(2,1)} %feat_hbm.1, bf16[3,32,3,8,128]{4,3,2,1,0:T(8,128)(2,1)} %edge_hbm.1, s32[3,8,128]{2,1,0:T(8,128)} %mult_hbm.1, bf16[3,32,96]{2,1,0:T(8,128)(2,1)} %win_hbm.1, bf16[3,32,32]{2,1,0:T(8,128)(2,1)} %wout_hbm.1, f32[3,32]{1,0:T(4,128)} %bin_hbm.1, ...), custom_call_target="tpu_custom_call" | custom-call | tf_op jit(solution)/shard_map/pallas_call | solution.py:485
  27.4 0.7 %copy.11 = bf16[32,3,8,128]{3,2,1,0:T(8,128)(2,1)} copy(bf16[32,3,8,128]{3,2,1,0:T(8,128)(2,1)S(1)} %shard_map.91) | data formatting | bytes 393216

commit v6 on v5

--- a/solution.py
+++ b/solution.py
@@ -12,7 +12,7 @@
 AXES = ("gx", "gy", "gz")
 F32, BF16 = jnp.float32, jnp.bfloat16
 STEPS = (-1, 0, 1)
-FAST, SLOW = 0, 1
+FAST, SLOW, MID = 0, 1, 2
 OTHER = 2
 
 
@@ -40,7 +40,7 @@
     out = []
     for way in ways_of(sizes):
         dx, dy, dz = way
-        out += [(way, tag) for tag in ((FAST, SLOW) if dx == 0 else (None,))]
+        out += [(way, tag) for tag in ((FAST, SLOW, MID) if dx == 0 else (None,))]
     return out
 
 
@@ -212,12 +212,13 @@
         if dz != 0:
             which = z_steps.index(dz)
             source = zsend.at[slot, which, SLOW if tag is None and face == slow else tag or FAST]
-            target = zrx.at[slot, which, {-1: 0, 0: 1 + (tag or 0), 1: 3}[dx], dy + 1]
+            target = zrx.at[slot, which, {-1: 0, 0: 1 + (tag or 0), 1: 4}[dx], dy + 1]
         elif dy == 0:
             source = p_s.at[slot, face]
             target = xrx.at[slot, 0 if dx < 0 else 1]
         elif dx == 0:
-            slabs = pl.ds(last - slow, 1) if tag == FAST else pl.ds(0 if slow == 0 else 1, last)
+            slabs = {FAST: (last - slow, 1), SLOW: (slow, 1), MID: (1, last - 1)}[tag]
+            slabs = pl.ds(*slabs)
             source = p_s.at[slot, slabs, :, edge_lanes(side)]
             target = yrx.at[slot, side, slabs]
         else:
@@ -255,8 +256,8 @@
                 )
                 piece = pltpu.roll(piece, at + 1, 1)
                 faces = jnp.where((lane == at) | (lane == at + 1), piece, faces)
-        turn_s[2] = faces.T
-        first, final = turn_s[2, odd_rows, :], turn_s[2, even_rows, :]
+        turn_s[3] = faces.T
+        first, final = turn_s[3, odd_rows, :], turn_s[3, even_rows, :]
         for which, dz in enumerate(z_steps):
             if dz == OTHER:
                 zsend[slot, which, phase] = jnp.where(place[2] == 0, final, first)
@@ -270,10 +271,11 @@
         shift_x = last * halves
         for dy in STEPS:
             part = zrx[slot, which, 1 + phase, dy + 1]
+            piece = 0.0
             if face == 0:
-                piece = zrx[slot, which, 3, dy + 1]
+                piece = zrx[slot, which, 4, dy + 1]
                 piece = jnp.where(row_z < halves, pltpu.roll(piece, zrows - shift_x, 0), 0.0)
-            else:
+            elif face == last:
                 piece = zrx[slot, which, 0, dy + 1]
                 inside = (row_z >= shift_x) & (row_z < shift_x + halves)
                 piece = jnp.where(inside, pltpu.roll(piece, shift_x, 0), 0.0)
@@ -359,9 +361,9 @@
                 if phase_of(message, True) == phase and (order(message) == (False, False)) == first:
                     start(message, slot, slow)
 
-        def arrivals(slot, phase, pick):
+        def arrivals(slot, phase):
             for message in ordered:
-                if phase_of(message, False) == phase and pick(message):
+                if phase_of(message, False) == phase:
                     arrive(message, slot, slow)
 
         def shared_edge(face):
@@ -403,14 +405,16 @@
 
         def layer_step(layer, carry):
             slot = layer
-            shared, *weighted = edges(layer, [shared_edge(slow)] + own_edges(slow))
-            put(slot, slow, shared + inside(weighted), False)
+            (shared,) = edges(layer, [shared_edge(slow)])
+            put_shared(slot, slow, shared)
+            z_faces(slot, middle, MID)
+            starts(slot, MID, False)
+            put(slot, slow, shared + inside(edges(layer, own_edges(slow))), False)
             starts(slot, SLOW, True)
-            put_shared(slot, slow, shared)
-            z_faces(slot, [slow] + middle, SLOW)
+            z_faces(slot, [slow], SLOW)
             starts(slot, SLOW, False)
 
-            arrivals(slot, FAST, lambda message: True)
+            arrivals(slot, FAST)
             columns = z_columns(slot, fast, FAST)
             keep_nodes(fast, node(layer, slot, fast, columns))
 
@@ -418,12 +422,8 @@
             def _():
                 fast_edges(layer + 1)
 
-            def late(message):
-                (dx, dy, dz), tag = message
-                return dz == 0 and dx != 0
-
-            arrivals(slot, SLOW, lambda message: not late(message))
-            columns = z_columns(slot, slow, SLOW)
+            arrivals(slot, MID)
+            columns = z_columns(slot, None, MID)
             for x in middle:
                 keep_nodes(x, node(layer, slot, x, columns))
 
@@ -434,7 +434,8 @@
 
             for message in messages:
                 sent(message, layer, slow)
-            arrivals(slot, SLOW, late)
+            arrivals(slot, SLOW)
+            columns = z_columns(slot, slow, SLOW)
             keep_nodes(slow, node(layer, slot, slow, columns))
             return carry
 
@@ -472,12 +473,12 @@
             pltpu.VMEM((slots, cx, chans, cells), F32),
             pltpu.VMEM((layers, chans, cz), F32),
             pltpu.VMEM((layers, chans, cz), F32),
-            pltpu.VMEM((slots, 2, 2, zrows, 128), F32),
+            pltpu.VMEM((slots, 2, 3, zrows, 128), F32),
             pltpu.VMEM((slots, 2, chans, cells), F32),
             pltpu.VMEM((slots, 2, cx, chans, cz), F32),
             pltpu.VMEM((slots, 4, chans, cz), F32),
-            pltpu.VMEM((slots, 2, 4, 3, zrows, 128), F32),
-            pltpu.VMEM((3, 128, 128), F32),
+            pltpu.VMEM((slots, 2, 5, 3, zrows, 128), F32),
+            pltpu.VMEM((4, 128, 128), F32),
             pltpu.SemaphoreType.DMA((9,)),
             pltpu.SemaphoreType.DMA((slots, ways)),
             pltpu.SemaphoreType.DMA((slots, ways)),

time: 28.2 us -> 27.6 us (0.979)
  Pallas kernels: 27.4 us -> 26.8 us
    pallas_call x1, Pallas kernels: 27.4 us -> 26.8 us  [on_device(): pl.pallas_call(functools.partial(kernel, sizes, layers), out_shape=pltpu....]
where the time goes in v6:
time: 27.6 us; the launch traced here: 27.4 us
  Pallas kernels  26.8 us (97%)
  local copies, waits for them, and re-layouts  0.68 us (2%)
    pallas_call x1, Pallas kernels, on_device(): pl.pallas_call(functools.partial(kernel, sizes, layers), out_shape=pltpu....  26.8 us
    unnamed x1, local copies, waits for them, and re-layouts  0.68 us

profile of v6, /device:TPU:1, one launch (start us, length us, event | category | flops | bytes accessed | tf_op | source)
XLA Modules:
  0.0 27.4 jit_solution(10656701500167756028)
XLA Ops:
  0.0 26.8 %shard_map.91 = bf16[32,3,8,128]{3,2,1,0:T(8,128)(2,1)S(1)} custom-call(bf16[32,3,8,128]{3,2,1,0:T(8,128)(2,1)} %feat_hbm.1, bf16[3,32,3,8,128]{4,3,2,1,0:T(8,128)(2,1)} %edge_hbm.1, s32[3,8,128]{2,1,0:T(8,128)} %mult_hbm.1, bf16[3,32,96]{2,1,0:T(8,128)(2,1)} %win_hbm.1, bf16[3,32,32]{2,1,0:T(8,128)(2,1)} %wout_hbm.1, f32[3,32]{1,0:T(4,128)} %bin_hbm.1, ...), custom_call_target="tpu_custom_call" | custom-call | tf_op jit(solution)/shard_map/pallas_call | solution.py:486
  26.8 0.7 %copy.11 = bf16[32,3,8,128]{3,2,1,0:T(8,128)(2,1)} copy(bf16[32,3,8,128]{3,2,1,0:T(8,128)(2,1)S(1)} %shard_map.91) | data formatting | bytes 393216

commit v7 on v6

--- a/solution.py
+++ b/solution.py
@@ -352,13 +352,14 @@
 
         def order(message):
             (dx, dy, dz), tag = message
-            return (dy != 0 or dz != 0, dz != 0)
+            hops = sum(step != 0 for step in (dx, dy, dz))
+            return (dz == 0, dz == 0 and dy != 0, -hops)
 
         ordered = sorted(messages, key=order)
 
-        def starts(slot, phase, first):
+        def starts(slot, phase):
             for message in ordered:
-                if phase_of(message, True) == phase and (order(message) == (False, False)) == first:
+                if phase_of(message, True) == phase:
                     start(message, slot, slow)
 
         def arrivals(slot, phase):
@@ -394,9 +395,8 @@
             put_shared(layer, fast, shared)
 
         def fast_sends(slot):
-            starts(slot, FAST, True)
             z_faces(slot, [fast], FAST)
-            starts(slot, FAST, False)
+            starts(slot, FAST)
 
         fast_edges(0)
         middle_edges(0)
@@ -408,11 +408,10 @@
             (shared,) = edges(layer, [shared_edge(slow)])
             put_shared(slot, slow, shared)
             z_faces(slot, middle, MID)
-            starts(slot, MID, False)
+            starts(slot, MID)
             put(slot, slow, shared + inside(edges(layer, own_edges(slow))), False)
-            starts(slot, SLOW, True)
             z_faces(slot, [slow], SLOW)
-            starts(slot, SLOW, False)
+            starts(slot, SLOW)
 
             arrivals(slot, FAST)
             columns = z_columns(slot, fast, FAST)

time: 27.6 us -> 26.7 us (0.967)
  Pallas kernels: 26.8 us -> 25.9 us
    pallas_call x1, Pallas kernels: 26.8 us -> 25.9 us  [on_device(): pl.pallas_call(functools.partial(kernel, sizes, layers), out_shape=pltpu....]
where the time goes in v7:
time: 26.7 us; the launch traced here: 26.6 us
  Pallas kernels  25.9 us (97%)
  local copies, waits for them, and re-layouts  0.68 us (3%)
    pallas_call x1, Pallas kernels, on_device(): pl.pallas_call(functools.partial(kernel, sizes, layers), out_shape=pltpu....  25.9 us
    unnamed x1, local copies, waits for them, and re-layouts  0.68 us

profile of v7, /device:TPU:1, one launch (start us, length us, event | category | flops | bytes accessed | tf_op | source)
XLA Modules:
  0.0 26.6 jit_solution(5563293441718019816)
XLA Ops:
  0.0 25.9 %shard_map.91 = bf16[32,3,8,128]{3,2,1,0:T(8,128)(2,1)S(1)} custom-call(bf16[32,3,8,128]{3,2,1,0:T(8,128)(2,1)} %feat_hbm.1, bf16[3,32,3,8,128]{4,3,2,1,0:T(8,128)(2,1)} %edge_hbm.1, s32[3,8,128]{2,1,0:T(8,128)} %mult_hbm.1, bf16[3,32,96]{2,1,0:T(8,128)(2,1)} %win_hbm.1, bf16[3,32,32]{2,1,0:T(8,128)(2,1)} %wout_hbm.1, f32[3,32]{1,0:T(4,128)} %bin_hbm.1, ...), custom_call_target="tpu_custom_call" | custom-call | tf_op jit(solution)/shard_map/pallas_call | solution.py:485
  25.9 0.7 %copy.11 = bf16[32,3,8,128]{3,2,1,0:T(8,128)(2,1)} copy(bf16[32,3,8,128]{3,2,1,0:T(8,128)(2,1)S(1)} %shard_map.91) | data formatting | bytes 393216

commit v8 on v7

--- a/solution.py
+++ b/solution.py
@@ -61,7 +61,7 @@
             (feat_hbm, feat_ref), (edge_hbm, edge_ref),
         ])
     ]
-    for load in loads:
+    for load in loads[::-1]:
         load.start()
 
     chans, cx, cy, cz = feat_ref.shape
@@ -107,7 +107,7 @@
     zrx[...] = jnp.zeros_like(zrx)
 
     barrier = pltpu.get_barrier_semaphore()
-    for way in ways:
+    for way in sorted(ways, key=lambda way: -sum(step != 0 for step in way)):
         def greet(way=way):
             pl.semaphore_signal(barrier, inc=1, device_id=device(way), device_id_type=MESH)
 

time: 26.7 us -> 26.8 us (level)
  no operation moved by 1% of the time
where the time goes in v8:
time: 26.8 us; the launch traced here: 26.7 us
  Pallas kernels  26 us (97%)
  local copies, waits for them, and re-layouts  0.68 us (3%)
    pallas_call x1, Pallas kernels, on_device(): pl.pallas_call(functools.partial(kernel, sizes, layers), out_shape=pltpu....  26 us
    unnamed x1, local copies, waits for them, and re-layouts  0.68 us

profile of v8, /device:TPU:1, one launch (start us, length us, event | category | flops | bytes accessed | tf_op | source)
XLA Modules:
  0.0 26.7 jit_solution(12478745831850489691)
XLA Ops:
  0.0 26.0 %shard_map.91 = bf16[32,3,8,128]{3,2,1,0:T(8,128)(2,1)S(1)} custom-call(bf16[32,3,8,128]{3,2,1,0:T(8,128)(2,1)} %feat_hbm.1, bf16[3,32,3,8,128]{4,3,2,1,0:T(8,128)(2,1)} %edge_hbm.1, s32[3,8,128]{2,1,0:T(8,128)} %mult_hbm.1, bf16[3,32,96]{2,1,0:T(8,128)(2,1)} %win_hbm.1, bf16[3,32,32]{2,1,0:T(8,128)(2,1)} %wout_hbm.1, f32[3,32]{1,0:T(4,128)} %bin_hbm.1, ...), custom_call_target="tpu_custom_call" | custom-call | tf_op jit(solution)/shard_map/pallas_call | solution.py:485
  26.0 0.7 %copy.11 = bf16[32,3,8,128]{3,2,1,0:T(8,128)(2,1)} copy(bf16[32,3,8,128]{3,2,1,0:T(8,128)(2,1)S(1)} %shard_map.91) | data formatting | bytes 393216
